TPU v7x, 32 devices: a whole 2x2x4 slice. The times are simulated.
32 devices in a mesh: groups: 2 (over y), replica: 8 (over z, x), tensor: 2 (over core).
Axes of the slice: x: 2, y: 2, z: 4, core: 2. Of those that a mesh axis runs over, the one named last changes fastest.
Arguments:
- hidden_states: bfloat16 [16384, 8192], P(('groups', 'replica'), 'tensor'), parts along dimension 0, may hold values from -6 to 6
- kv_weight: bfloat16 [8192, 2, 1024], P('tensor'), may hold values from -0.0625 to 0.0625
- pool_down: bfloat16 [32, 8192, 2, 128], P(('groups', 'replica'), 'tensor'), parts along dimension 0, may hold values from -0.0625 to 0.0625
- pool_up: bfloat16 [32, 2, 128, 1024], P(('groups', 'replica'), None, None, 'tensor'), parts along dimension 0, may hold values from -3 to 3
- adapter_rank: int32 [32], P('groups'), parts along dimension 0, may hold values from 16 to 128, as said below
- pool_row: int32 [32], P('groups'), parts along dimension 0, may hold values from 0 to 15, as said below
- request_adapter: int32 [16, 8], P(('groups', 'replica')), parts along dimension 0, may hold values from 0 to 15, as said below
- request_length: int32 [16, 8], P(('groups', 'replica')), parts along dimension 0, may hold values from 1 to 512, 1024 in all within a row
Outputs:
- keys: bfloat16 [16384, 1024], P(('groups', 'replica'), 'tensor'), parts along dimension 0
- values: bfloat16 [16384, 1024], P(('groups', 'replica'), 'tensor'), parts along dimension 0
There are 2 independent parts, one for each index of `groups`. A program takes and returns all parts, laid end to end along the dimension named above; an argument that names none is the same for every part. Nothing has to cross between parts.
Inputs may be any that keep to these rules, and one draw needn't show every extreme that they name: `pool_row`: a permutation: every pool row holds one adapter. `adapter_rank`: each of 16, 32, 64 and 128; some adapter has rank 128. `request_adapter`: at most 1 request of one replica index name adapters held in the pool rows of any one replica index (rows q * 2 to (q+1) * 2 - 1 belong to index q), and some replica index reaches 1 from some index.
All inputs are finite; a program needn't handle non-finite values.
Results may differ from a plain program's by a relative error of at most 0.0095.
Values may be sent and summed in bfloat16 or wider, within the bound.
No kernel may reach another device: no remote copies, remote signals or barrier semaphores. Data moves between devices by JAX's collectives and lax.ppermute only.
A program may use at most 256 MiB of HBM per device.

v0:
```python
import jax
import jax.numpy as jnp
from jax import lax
from jax.sharding import PartitionSpec as P


def table_lookup(indices, table):
    return jnp.sum(
        jnp.where(
            indices[:, None] == jnp.arange(table.shape[0], dtype=jnp.int32)[None, :],
            table[None, :],
            0,
        ),
        axis=1,
    )


def per_device(
    hidden_states,
    kv_weight,
    pool_down,
    pool_up,
    adapter_rank,
    pool_row,
    request_adapter,
    request_length,
):
    tok_rows, width_dev = hidden_states.shape
    kv_cols = kv_weight.shape[2]
    rank_max = pool_down.shape[3]
    count = request_length.shape[1]
    lengths = request_length[0]
    request_end = jnp.cumsum(lengths)
    adapters = request_adapter[0]
    rows_of = table_lookup(adapters, pool_row)
    ranks = table_lookup(adapters, adapter_rank)
    partial_value = jnp.dot(
        hidden_states, kv_weight.reshape(width_dev, 2 * kv_cols), preferred_element_type=jnp.float32
    )
    base = lax.psum_scatter(
        partial_value.reshape(tok_rows, 2, kv_cols).astype(jnp.bfloat16),
        "tensor",
        scatter_dimension=2,
        tiled=True,
    ).astype(jnp.float32)
    down_piece = lax.all_gather(pool_down, "replica", axis=0, tiled=True)
    up_piece = lax.all_gather(pool_up, "replica", axis=0, tiled=True)
    numbered = jnp.arange(down_piece.shape[0], dtype=jnp.int32)
    onehot = (rows_of[:, None] == numbered[None, :]).astype(jnp.bfloat16)
    picked_down = jnp.einsum(
        "jn,nabc->jabc", onehot, down_piece, preferred_element_type=jnp.float32
    )
    picked_up = jnp.einsum("jn,nabc->jabc", onehot, up_piece, preferred_element_type=jnp.float32)
    down_req = picked_down.astype(jnp.bfloat16)
    up_req = picked_up.astype(jnp.bfloat16)
    column = jnp.arange(rank_max, dtype=jnp.int32)
    rank_scale = jnp.where(
        column[None, :] < ranks[:, None], 1.0 / jnp.sqrt(ranks.astype(jnp.float32))[:, None], 0.0
    )
    token_pos = jnp.arange(tok_rows, dtype=jnp.int32)
    token_request = jnp.sum((token_pos[:, None] >= request_end[None, :]).astype(jnp.int32), axis=1)
    onehot_req = (token_request[:, None] == jnp.arange(count, dtype=jnp.int32)[None, :]).astype(
        jnp.float32
    )
    token_scale = jnp.dot(onehot_req, rank_scale, precision=lax.Precision.HIGHEST)
    shrink = lax.ragged_dot(
        hidden_states,
        down_req.reshape(count, width_dev, 2 * rank_max),
        lengths,
        preferred_element_type=jnp.float32,
    ).reshape(tok_rows, 2, rank_max)
    shrink = (shrink * token_scale[:, None, :]).reshape(tok_rows, 2 * rank_max)
    summed = lax.psum(shrink.astype(jnp.bfloat16), "tensor")
    key_delta = lax.ragged_dot(
        summed[:, :rank_max], up_req[:, 0], lengths, preferred_element_type=jnp.float32
    )
    value_delta = lax.ragged_dot(
        summed[:, rank_max:], up_req[:, 1], lengths, preferred_element_type=jnp.float32
    )
    keys = (base[:, 0] + key_delta).astype(jnp.bfloat16)
    values = (base[:, 1] + value_delta).astype(jnp.bfloat16)
    return (keys, values)


def solution(mesh):
    placed = (
        P(("groups", "replica"), "tensor"),
        P("tensor", None, None),
        P(("groups", "replica"), "tensor", None, None),
        P(("groups", "replica"), None, None, "tensor"),
        P("groups"),
        P("groups"),
        P(("groups", "replica"), None),
        P(("groups", "replica"), None),
    )
    return jax.shard_map(
        per_device,
        mesh=mesh,
        in_specs=placed,
        out_specs=(P(("groups", "replica"), "tensor"), P(("groups", "replica"), "tensor")),
        check_vma=False,
    )
```

profile of v0, /device:TPU:0, one launch (start us, length us, event | category | flops | bytes accessed | tf_op | source)
XLA Modules:
  0.0 854.2 jit_solution(6223662847262131591)
XLA Ops:
  8.0 0.0 all-gather.3.cloned.1.call-start
  8.0 4.7 copy.22
  12.7 0.0 all-gather.3.cloned.1.call-update
  12.7 0.0 all-gather.5.cloned.1.call-start
  12.8 0.7 all-gather.5.cloned.1.call-update
  13.5 0.0 reduce-scatter.2.cloned.1.call-start
  13.6 17.2 %copy.28 = bf16[512,8,2,1024]{3,1,2,0:T(8,128)(2,1)} copy(bf16[512,8,2,1024]{3,2,1,0:T(2,128)(2,1)} %bitcast.43) | data formatting | bytes 33554432
  30.8 20.7 %copy.21 = bf16[2048,4096]{1,0:T(8,128)(2,1)} copy(bf16[2048,4096]{0,1:T(8,128)(2,1)} %bitcast.42) | data formatting | bytes 33554432 | tf_op jit(solution)/shard_map/dot_general | solution.py:37
  51.4 23.9 %fusion.9 = bf16[1024,2,1024]{2,0,1:T(8,128)(2,1)} fusion(bf16[2,1024,4096]{2,1,0:T(8,128)(2,1)} %bitcast.44, bf16[1024,4096]{1,0:T(8,128)(2,1)} %param.8), kind=kOutput, calls=%fused_computation.8 | convolution fusion | flops 17181966336 | bytes 29360128 | tf_op jit(solution)/shard_map/dot_general | solution.py:37
  75.3 0.0 copy-start.4
  75.3 0.0 copy-start.1
  75.3 0.0 copy-start.2
  75.3 0.0 copy-start.3
  75.3 0.0 reduce-scatter.2.cloned.1.call-update
  75.3 0.0 all-reduce.2.cloned.1.call-start
  75.4 1.5 ragged-dot-metadata
  76.9 0.0 copy-done.4
  76.9 0.2 reduce-window.8
  77.1 0.1 convert_reduce_fusion
  77.2 0.0 copy-done.1
  77.2 0.0 copy-done.2
  77.2 0.0 copy-done.3
  77.2 0.2 select_reduce_fusion
  77.4 0.5 fusion.17
  77.9 575.4 %all-gather.3.cloned.1.call-done = bf16[16,4096,2,128]{3,1,2,0:T(8,128)(2,1)} async-done(((bf16[2,4096,2,128]{3,1,2,0:T(8,128)(2,1)}), bf16[16,4096,2,128]{3,1,2,0:T(8,128)(2,1)}) %all-gather.3.cloned.1.call-update) | async-done | bytes 33554448 | tf_op jit(solution)/shard_map/all_gather | solution.py:46
  653.3 76.4 %fusion.2 = bf16[8,4096,2,128]{3,0,2,1:T(8,128)(2,1)} fusion(bf16[16,4096,2,128]{3,1,2,0:T(8,128)(2,1)} %all-gather.3.cloned.1.call-done, s32[8]{0:T(128)S(1)} %get-tuple-element.15), kind=kOutput, calls=%fused_computation.2 | convolution fusion | flops 276824192 | bytes 50331680 | tf_op jit(solution)/shard_map/jn,nabc->jabc/dot_general | solution.py:50
  729.7 24.4 %copy.24 = bf16[8,4096,2,128]{3,2,1,0:T(2,128)(2,1)} copy(bf16[8,4096,2,128]{3,0,2,1:T(8,128)(2,1)} %fusion.2) | data formatting | bytes 33554432 | tf_op jit(solution)/shard_map/convert_element_type | solution.py:54
  754.1 26.9 %reshape.52 = bf16[8,4096,256]{2,1,0:T(8,128)(2,1)} reshape(bf16[8,4096,2,128]{3,2,1,0:T(2,128)(2,1)} %copy.24) | data formatting | bytes 33554432 | tf_op jit(solution)/shard_map/reshape | solution.py:68
  781.0 17.7 %ragged-dot-none.2 = f32[1024,256]{1,0:T(8,128)} custom-call(s32[1]{0:T(128)} %get-tuple-element.6, s32[9]{0:T(128)} %get-tuple-element.7, s32[11]{0:T(128)} %get-tuple-element.8, s32[11]{0:T(128)} %get-tuple-element.9, s32[1]{0:T(128)} %get-tuple-element.6, bf16[1024,4096]{1,0:T(8,128)(2,1)} %param.8, bf16[8,4096,256]{2,1,0:T(8,128)(2,1)} %reshape.52), custom_call_target="tpu_custom_call" | custom-call | flops 2147483648 | bytes 26214432 | tf_op jit(solution)/shard_map/ragged_dot_general/ragged-dot-none
  798.8 0.4 mul.11
  799.1 2.2 fusion.16
  801.3 0.0 all-reduce.2.cloned.1.call-update
  801.3 0.0 all-gather.5.cloned.1.call-done
  801.3 4.6 fusion.7
  806.0 0.7 copy.38
  806.7 1.5 slice_bitcast_fusion.2
  808.2 0.0 reduce-scatter.2.cloned.1.call-done
  808.2 4.2 convert_element_type.34
  812.4 7.3 all-reduce.2.cloned.1.call-done
  819.7 1.9 fusion.29
  821.7 10.0 %ragged-dot-none.1 = f32[1024,512]{1,0:T(8,128)} custom-call(s32[1]{0:T(128)} %get-tuple-element.6, s32[9]{0:T(128)} %get-tuple-element.7, s32[11]{0:T(128)} %get-tuple-element.8, s32[11]{0:T(128)} %get-tuple-element.9, s32[1]{0:T(128)} %get-tuple-element.6, bf16[1024,128]{1,0:T(8,128)(2,1)} %get-tuple-element.21, bf16[8,128,512]{2,1,0:T(8,128)(2,1)} %get-tuple-element.19), custom_call_target="tpu_custom_call" | custom-call | flops 134217728 | bytes 3407904 | tf_op jit(solution)/shard_map/ragged_dot_general/ragged-dot-none
  831.6 0.0 copy-start
  831.6 10.1 %ragged-dot-none = f32[1024,512]{1,0:T(8,128)} custom-call(s32[1]{0:T(128)} %get-tuple-element.6, s32[9]{0:T(128)} %get-tuple-element.7, s32[11]{0:T(128)} %get-tuple-element.8, s32[11]{0:T(128)} %get-tuple-element.9, s32[1]{0:T(128)} %get-tuple-element.6, bf16[1024,128]{1,0:T(8,128)(2,1)} %get-tuple-element.20, bf16[8,128,512]{2,1,0:T(8,128)(2,1)} %get-tuple-element.18), custom_call_target="tpu_custom_call" | custom-call | flops 134217728 | bytes 3407904 | tf_op jit(solution)/shard_map/ragged_dot_general/ragged-dot-none
  841.7 0.0 copy-done
  841.7 4.9 fusion.13
  (1 shorter events, 0.0 us)
Async XLA Ops:
  8.0 645.3 %all-gather.3.cloned.1.call-start = ((), (), s32[]{:S(2)}) async-start(), calls=%async_computation.2 | async-start | bytes 37748736 | tf_op jit(solution)/shard_map/all_gather | solution.py:46
  12.7 788.6 %all-gather.5.cloned.1.call-start = ((), (), s32[]{:S(2)}) async-start(), calls=%async_computation.4 | async-start | bytes 4718592 | tf_op jit(solution)/shard_map/all_gather | solution.py:47
  13.5 794.7 %reduce-scatter.2.cloned.1.call-start = ((), (), s32[]{:S(2)}) async-start(), calls=%async_computation.1 | async-start | bytes 6291456 | tf_op jit(solution)/shard_map/reduce_scatter | solution.py:40
  75.3 1.6 copy-start.4
  75.3 1.9 copy-start.1
  75.3 1.9 copy-start.2
  75.3 1.9 copy-start.3
  75.3 744.4 %all-reduce.2.cloned.1.call-start = ((), (), s32[]{:S(2)}) async-start(), calls=%async_computation.3 | async-start | bytes 1048576 | tf_op jit(solution)/shard_map/psum | solution.py:73
  831.6 10.1 %copy-start = (f32[1024,512]{1,0:T(8,128)S(1)}, f32[1024,512]{1,0:T(8,128)}, u32[]{:S(2)}) copy-start(f32[1024,512]{1,0:T(8,128)} %ragged-dot-none.1) | copy-start | bytes 6291460
Sparse Core Ops, SparseCore 0:
  12.9 640.4 all-gather.2
  655.5 73.3 all-gather.4
Sparse Core Ops, SparseCore 1:
  75.4 14.6 reduce-scatter.1
  801.4 18.3 all-reduce.1
where the time goes:
time: 867 us; the launch traced here: 854 us
  waiting for transfers between devices  584 us (67%)
  matrix products  105 us (12%)
  local copies, waits for them, and re-layouts  98.4 us (11%)
  Pallas kernels  39.3 us (5%)
  between operations  15.8 us (2%)
  other arithmetic  11.7 us (1%)
    all_gather x1, waiting for transfers between devices, per_device(): down_piece = lax.all_gather(pool_down, 'replica', axis=0, tiled=True)  575 us
    dot_general x1, matrix products, per_device(): jnp.einsum('jn,nabc->jabc', onehot, down_piece, preferred_element_type=jn...  76.4 us
    another operation x3, Pallas kernels  37.8 us
    reshape x1, local copies, waits for them, and re-layouts, per_device(): down_req.reshape(count, width_dev, 2 * rank_max)  26.9 us
    convert_element_type x1, local copies, waits for them, and re-layouts, per_device(): down_req = picked_down.astype(jnp.bfloat16)  24.4 us
    dot_general x1, matrix products, per_device(): jnp.dot(hidden_states, kv_weight.reshape(width_dev, 2 * kv_cols), preferr...  23.9 us
    unnamed x12, local copies, waits for them, and re-layouts  21.9 us
    dot_general x1, local copies, waits for them, and re-layouts, per_device(): jnp.dot(hidden_states, kv_weight.reshape(width_dev, 2 * kv_cols), preferr...  20.7 us
  transfers between devices with their start and end apart: 4, of which 2 were waited for; matrix products, arithmetic and copies ran while one was open for 24% of the time, Pallas kernels for 2%

commit v1 on v0

v1 whole, which is shorter than its diff:
```python
import functools

import jax
import jax.numpy as jnp
from jax import lax
from jax.experimental import pallas as pl
from jax.experimental.pallas import tpu as pltpu
from jax.sharding import PartitionSpec as P

TILE = 128
BF16 = jnp.bfloat16
F32 = jnp.float32


def table_lookup(indices, table):
    hit = indices[:, None] == jnp.arange(table.shape[0], dtype=jnp.int32)[None, :]
    return jnp.sum(jnp.where(hit, table[None, :], 0), axis=1)


def visit_list(lengths, slots, ranks, rows):
    count = lengths.shape[0]
    steps = rows // TILE + count - 1
    ends = jnp.cumsum(lengths)
    starts = ends - lengths
    first = starts // TILE
    tiles = (ends - 1) // TILE - first + 1
    upto = jnp.cumsum(tiles)
    step = jnp.arange(steps, dtype=jnp.int32)
    live = step < upto[-1]
    request = jnp.minimum(jnp.sum((step[:, None] >= upto[None, :]).astype(jnp.int32), axis=1), count - 1)
    pick = lambda t: table_lookup(request, t)
    tile = jnp.where(live, pick(first) + step - pick(upto - tiles), rows // TILE - 1)
    begin = jnp.where(live, pick(starts), 0)
    end = jnp.where(live, pick(ends), 0)
    return tile, pick(slots), begin, end, pick(ranks)


def shrink_kernel(tile, slot, begin, end, rank, scale, h_ref, d_ref, o_ref):
    i = pl.program_id(0)
    top = tile[i] * TILE
    grown = jnp.dot(h_ref[...], d_ref[0], preferred_element_type=F32) * scale[i]
    row = lax.broadcasted_iota(jnp.int32, grown.shape, 0) + top
    col = lax.broadcasted_iota(jnp.int32, grown.shape, 1)
    half = grown.shape[1] // 2
    col = jnp.where(col >= half, col - half, col)
    mine = (row >= begin[i]) & (row < end[i])
    value = jnp.where(col < rank[i], grown, 0.0)
    fresh = jnp.logical_or(i == 0, tile[i] != tile[jnp.maximum(i - 1, 0)])

    @pl.when(fresh)
    def _():
        o_ref[...] = jnp.where(mine, value, 0.0).astype(o_ref.dtype)

    @pl.when(jnp.logical_not(fresh))
    def _():
        o_ref[...] = jnp.where(mine, value, o_ref[...].astype(F32)).astype(o_ref.dtype)


def shrink_call(visits, scale, tokens, downs):
    tile, slot, begin, end, rank = visits
    rows, width = tokens.shape
    cols = downs.shape[2]
    steps = tile.shape[0]
    return pl.pallas_call(
        shrink_kernel,
        grid_spec=pltpu.PrefetchScalarGridSpec(
            num_scalar_prefetch=6,
            grid=(steps,),
            in_specs=[
                pl.BlockSpec((TILE, width), lambda i, t, s, *_: (t[i], 0)),
                pl.BlockSpec((1, width, cols), lambda i, t, s, *_: (s[i], 0, 0)),
            ],
            out_specs=pl.BlockSpec((TILE, cols), lambda i, t, s, *_: (t[i], 0)),
        ),
        out_shape=jax.ShapeDtypeStruct((rows, cols), BF16),
        compiler_params=pltpu.CompilerParams(
            dimension_semantics=("arbitrary",), vmem_limit_bytes=32 * 2**20
        ),
        cost_estimate=pl.CostEstimate(
            flops=2 * steps * TILE * width * cols, bytes_accessed=2 * rows * width * 2, transcendentals=0
        ),
    )(tile, slot, begin, end, rank, scale, tokens, downs)


def grow_kernel(tile, slot, begin, end, rank, s_ref, u_ref, own_ref, other_ref, k_ref, v_ref, acc):
    i = pl.program_id(0)
    steps = pl.num_programs(0)
    top = tile[i] * TILE
    half = s_ref.shape[1] // 2
    feat = k_ref.shape[1]
    row = lax.broadcasted_iota(jnp.int32, (TILE, half), 0) + top
    mine = (row >= begin[i]) & (row < end[i])
    fresh = jnp.logical_or(i == 0, tile[i] != tile[jnp.maximum(i - 1, 0)])

    @pl.when(fresh)
    def _():
        acc[...] = own_ref[...].astype(F32) + other_ref[...].astype(F32)

    for kv in range(2):
        part = s_ref[:, kv * half : (kv + 1) * half]
        part = jnp.where(mine, part.astype(F32), 0.0).astype(BF16)
        cols = slice(kv * feat, (kv + 1) * feat)
        acc[:, cols] += jnp.dot(part, u_ref[0, kv], preferred_element_type=F32)
    last = jnp.logical_or(i == steps - 1, tile[i] != tile[jnp.minimum(i + 1, steps - 1)])

    @pl.when(last)
    def _():
        k_ref[...] = acc[:, :feat].astype(BF16)
        v_ref[...] = acc[:, feat:].astype(BF16)


def grow_call(visits, shrunk, ups, own, other):
    tile, slot, begin, end, rank = visits
    rows, cols = shrunk.shape
    feat = ups.shape[3]
    steps = tile.shape[0]
    by_tile = lambda i, t, *_: (t[i], 0)
    return pl.pallas_call(
        grow_kernel,
        grid_spec=pltpu.PrefetchScalarGridSpec(
            num_scalar_prefetch=5,
            grid=(steps,),
            in_specs=[
                pl.BlockSpec((TILE, cols), by_tile),
                pl.BlockSpec((1,) + ups.shape[1:], lambda i, t, s, *_: (s[i], 0, 0, 0)),
                pl.BlockSpec((TILE, 2 * feat), by_tile),
                pl.BlockSpec((TILE, 2 * feat), by_tile),
            ],
            out_specs=[pl.BlockSpec((TILE, feat), by_tile)] * 2,
            scratch_shapes=[pltpu.VMEM((TILE, 2 * feat), F32)],
        ),
        out_shape=[jax.ShapeDtypeStruct((rows, feat), BF16)] * 2,
        compiler_params=pltpu.CompilerParams(
            dimension_semantics=("arbitrary",), vmem_limit_bytes=32 * 2**20
        ),
        cost_estimate=pl.CostEstimate(
            flops=2 * steps * TILE * cols * feat, bytes_accessed=6 * rows * feat * 2, transcendentals=0
        ),
    )(tile, slot, begin, end, rank, shrunk, ups, own, other)


def per_device(
    replicas,
    cores,
    hidden_states,
    kv_weight,
    pool_down,
    pool_up,
    adapter_rank,
    pool_row,
    request_adapter,
    request_length,
):
    rows, width = hidden_states.shape
    kv_cols = kv_weight.shape[2]
    held, rank_max = pool_down.shape[0], pool_down.shape[3]
    team = 4 if replicas % 4 == 0 else 1
    part = width // team
    me = lax.axis_index("replica")
    core = lax.axis_index("tensor")

    def swap(x, o):
        return lax.ppermute(x, "replica", [(i, i ^ o) for i in range(replicas)])

    def other_core(x):
        return lax.ppermute(x, "tensor", [(0, 1), (1, 0)])

    wanted = table_lookup(request_adapter[0], pool_row)
    table = lax.all_gather(jnp.concatenate([wanted, request_length[0]])[None], "replica", axis=0, tiled=True)
    count = request_length.shape[1]
    place = jnp.arange(pool_row.shape[0], dtype=jnp.int32)
    row_rank = jnp.sum(jnp.where(pool_row[None, :] == place[:, None], adapter_rank[None, :], 0), axis=1)

    def facts(o):
        line = lax.dynamic_slice_in_dim(table, me ^ o, 1, 0)[0]
        return line[:count], line[count:]

    downs = pool_down.reshape(held, width, 2 * rank_max)

    def share(x, axis, o):
        return lax.dynamic_slice_in_dim(x, ((me ^ o) % team) * part, part, axis)

    down_all = [share(downs, 1, 0)] + [swap(share(downs, 1, o), o) for o in range(1, replicas)]
    down_all = jnp.concatenate(down_all, axis=0)
    tokens = [share(hidden_states, 1, 0)] + [swap(share(hidden_states, 1, o), o) for o in range(1, team)]
    tokens = jnp.concatenate(tokens, axis=0)

    product = jnp.dot(
        hidden_states, kv_weight.reshape(width, 2 * kv_cols), preferred_element_type=F32
    ).astype(BF16)
    feat = kv_cols // cores
    if cores == 2:

        def features(c):
            return jnp.concatenate(
                [lax.dynamic_slice_in_dim(product, kv * kv_cols + c * feat, feat, 1) for kv in range(2)], axis=1
            )

        base_own = features(core)
        base_other = other_core(features(1 - core))
    else:
        base_own = jnp.concatenate(
            [
                lax.psum_scatter(
                    product[:, kv * kv_cols : (kv + 1) * kv_cols], "tensor", scatter_dimension=1, tiled=True
                )
                for kv in range(2)
            ],
            axis=1,
        )
        base_other = jnp.zeros_like(base_own)

    def upper(o):
        need, _ = facts(o)
        slot = jnp.sum(jnp.where(need // held == me, need % held, 0))
        return lax.dynamic_slice_in_dim(pool_up, slot, 1, 0)

    ups = jnp.concatenate([upper(0)] + [swap(upper(o), o) for o in range(1, replicas)], axis=0)

    down_all, tokens, ups, base_own, base_other = lax.optimization_barrier(
        (down_all, tokens, ups, base_own, base_other)
    )

    visits = []
    for o in range(team):
        need, lengths = facts(o)
        slots = ((need // held) ^ me) * held + need % held
        ranks = table_lookup(need, row_rank)
        tile, slot, begin, end, rank = visit_list(lengths, slots, ranks, rows)
        visits.append((tile + o * (rows // TILE), slot, begin + o * rows, end + o * rows, rank))
    visits = [jnp.concatenate(v) for v in zip(*visits)]
    scale = 1.0 / jnp.sqrt(visits[4].astype(F32))
    partial = shrink_call(visits, scale, tokens, down_all).reshape(team, rows, 2 * rank_max)
    if cores == 2:
        keep = lax.dynamic_slice_in_dim(partial, core * rank_max, rank_max, 2)
        give = lax.dynamic_slice_in_dim(partial, (1 - core) * rank_max, rank_max, 2)
        partial = (keep.astype(F32) + other_core(give).astype(F32)).astype(BF16)
    else:
        partial = lax.psum(partial, "tensor")
    total = partial[0].astype(F32)
    for o in range(1, team):
        total = total + swap(partial[o], o).astype(F32)
    shrunk = total.astype(BF16)
    if cores == 2:
        peer = other_core(shrunk)
        shrunk = jnp.concatenate(
            [jnp.where(core == 0, shrunk, peer), jnp.where(core == 0, peer, shrunk)], axis=1
        )

    need, lengths = facts(0)
    own_visits = visit_list(lengths, (need // held) ^ me, table_lookup(need, row_rank), rows)
    keys, values = grow_call(own_visits, shrunk, ups, base_own, base_other)
    return keys, values


def solution(mesh):
    placed = (
        P(("groups", "replica"), "tensor"),
        P("tensor", None, None),
        P(("groups", "replica"), "tensor", None, None),
        P(("groups", "replica"), None, None, "tensor"),
        P("groups"),
        P("groups"),
        P(("groups", "replica"), None),
        P(("groups", "replica"), None),
    )
    return jax.shard_map(
        functools.partial(per_device, mesh.shape["replica"], mesh.shape["tensor"]),
        mesh=mesh,
        in_specs=placed,
        out_specs=(P(("groups", "replica"), "tensor"), P(("groups", "replica"), "tensor")),
        check_vma=False,
    )
```

time: 867 us -> 436 us (0.50); the launches traced: 854 us -> 434 us
  waiting for transfers between devices: 584 us -> 235 us
  matrix products: 105 us -> 24.6 us
  local copies, waits for them, and re-layouts: 98.4 us -> 63.7 us
  starting transfers between devices: 0.17 us -> 32.1 us
  Pallas kernels: 39.3 us -> 23.3 us
  other arithmetic: 11.7 us -> 25.9 us
  blocking collectives: 0 us -> 13.1 us
    all_gather x2 -> x0, waiting for transfers between devices: 575 us -> none  [the longest x1 575 us: per_device(): down_piece = lax.all_gather(pool_down, 'replica', axis=0, tiled=True)]
    ppermute x0 -> x23, waiting for transfers between devices: none -> 235 us  [the longest x20 231 us: swap(): return lax.ppermute(x, 'replica', [(i, i ^ o) for i in range(replicas)])]
    dot_general x4 -> x1, matrix products: 105 us -> 24.6 us  [per_device(): jnp.dot(hidden_states, kv_weight.reshape(width, 2 * kv_cols), preferred_e...]
    another operation x3 -> x0, Pallas kernels: 37.8 us -> none
    ppermute x0 -> x23, starting transfers between devices: none -> 32.1 us  [the longest x20 31.9 us: swap(): return lax.ppermute(x, 'replica', [(i, i ^ o) for i in range(replicas)])]
    convert_element_type x1 -> x0, local copies, waits for them, and re-layouts: 24.4 us -> none  [per_device(): down_req = picked_down.astype(jnp.bfloat16)]
    pallas_call x0 -> x2, Pallas kernels: none -> 23.3 us  [the longest x1 16.2 us: shrink_call(): pl.pallas_call(shrink_kernel, grid_spec=pltpu.PrefetchScalarGridSpec(num_...]
    dot_general x2 -> x0, local copies, waits for them, and re-layouts: 21.4 us -> none  [the longest x1 20.7 us: per_device(): jnp.dot(hidden_states, kv_weight.reshape(width_dev, 2 * kv_cols), preferr...]
  transfers between devices with their start and end apart: 4 -> 23, of which waited for: 2 -> 9; matrix products, arithmetic and copies ran while one was open for 24% -> 22% of each run, Pallas kernels for 2% -> 0%
where the time goes in v1:
time: 436 us; the launch traced here: 434 us
  waiting for transfers between devices  235 us (54%)
  local copies, waits for them, and re-layouts  63.7 us (15%)
  starting transfers between devices  32.1 us (7%)
  other arithmetic  25.9 us (6%)
  matrix products  24.6 us (6%)
  Pallas kernels  23.3 us (5%)
  between operations  17 us (4%)
  blocking collectives  13.1 us (3%)
    ppermute x20, waiting for transfers between devices, swap(): return lax.ppermute(x, 'replica', [(i, i ^ o) for i in range(replicas)])  231 us
    unnamed x67, local copies, waits for them, and re-layouts  38.2 us
    ppermute x20, starting transfers between devices, swap(): return lax.ppermute(x, 'replica', [(i, i ^ o) for i in range(replicas)])  31.9 us
    dot_general x1, matrix products, per_device(): jnp.dot(hidden_states, kv_weight.reshape(width, 2 * kv_cols), preferred_e...  24.6 us
    pallas_call x1, Pallas kernels, shrink_call(): pl.pallas_call(shrink_kernel, grid_spec=pltpu.PrefetchScalarGridSpec(num_...  16.2 us
    unnamed x1, blocking collectives  13.1 us
  transfers between devices with their start and end apart: 23, of which 9 were waited for; matrix products, arithmetic and copies ran while one was open for 22% of the time, Pallas kernels for 0%

profile of v1, /device:TPU:0, one launch (start us, length us, event | category | flops | bytes accessed | tf_op | source)
XLA Modules:
  0.0 434.5 jit_solution(16213658863232816643)
XLA Ops:
  0.7 1.2 dynamic-slice
  4.2 13.1 %all-reduce = s32[128]{0:T(128)S(1)} all-reduce(s32[128]{0:T(128)S(1)} %add_dynamic-update-slice_fusion), channel_id=2, replica_groups=mesh['groups'=2,'replica'=8,'tensor'=2] {'replica'}, use_global_device_ids=true, to_apply=%add | all-reduce | flops 128 | bytes 1024
  35.3 2.9 constant_dynamic-slice_fusion.5
  38.1 1.6 collective-permute-start.10
  40.1 1.5 collective-permute-start.12
  42.0 3.7 collective-permute-start.14
  50.4 7.6 %reshape.827 = bf16[2,4096,256]{2,1,0:T(8,128)(2,1)} reshape(bf16[2,4096,2,128]{3,2,1,0:T(2,128)(2,1)} %param.10) | data formatting | bytes 8388608 | tf_op jit(solution)/shard_map/reshape | solution.py:178
  58.1 17.1 %copy.10 = bf16[512,8,2,1024]{3,1,2,0:T(8,128)(2,1)} copy(bf16[512,8,2,1024]{3,2,1,0:T(2,128)(2,1)} %bitcast.190) | data formatting | bytes 33554432
  79.8 24.6 %convolution_convert_fusion = bf16[1024,2048]{1,0:T(8,128)(2,1)} fusion(bf16[1024,4096]{1,0:T(8,128)(2,1)} %param.8, bf16[4096,2048]{1,0:T(8,128)(2,1)} %bitcast.191), kind=kOutput, calls=%fused_computation.1 | convolution fusion | flops 17181966336 | bytes 29360128 | tf_op jit(solution)/shard_map/dot_general | solution.py:188
  105.8 4.1 constant_dynamic-slice_fusion.19
  110.6 3.4 constant_dynamic-slice_fusion.20
  116.1 2.6 collective-permute-start.2
  118.9 2.5 collective-permute-start.15
  121.4 3.5 constant_dynamic-slice_fusion.2
  125.5 67.3 %collective-permute-done.15 = bf16[1,2,128,512]{3,2,1,0:T(8,128)(2,1)S(1)} collective-permute-done((bf16[1,2,128,512]{3,2,1,0:T(8,128)(2,1)}, bf16[1,2,128,512]{3,2,1,0:T(8,128)(2,1)S(1)}, u32[]{:S(2)}, u32[]{:S(2)}) %collective-permute-start.15) | collective-permute-done | bytes 262176 | tf_op jit(solution)/shard_map/ppermute | solution.py:163
  192.9 4.2 collective-permute-start.16
  197.8 6.2 %collective-permute-done.16 = bf16[1,2,128,512]{3,2,1,0:T(8,128)(2,1)S(1)} collective-permute-done((bf16[1,2,128,512]{3,2,1,0:T(8,128)(2,1)S(1)}, bf16[1,2,128,512]{3,2,1,0:T(8,128)(2,1)S(1)}, u32[]{:S(2)}, u32[]{:S(2)}) %collective-permute-start.16) | collective-permute-done | bytes 262176 | tf_op jit(solution)/shard_map/ppermute | solution.py:163
  204.8 1.7 pad_maximum_fusion.2
  206.5 2.7 collective-permute-start.5
  209.3 3.0 collective-permute-start.7
  212.4 1.5 collective-permute-start.9
  214.2 3.0 pad_maximum_fusion.1.own_ref
  217.1 1.1 constant_dynamic-update-slice_fusion.13
  218.2 1.0 constant_dynamic-update-slice_fusion.12
  220.1 49.5 %collective-permute-done.4 = bf16[2,1024,256]{2,1,0:T(8,128)(2,1)} collective-permute-done((bf16[2,1024,256]{2,1,0:T(8,128)(2,1)}, bf16[2,1024,256]{2,1,0:T(8,128)(2,1)}, u32[]{:S(2)}, u32[]{:S(2)}) %collective-permute-start.4) | collective-permute-done | bytes 1048608 | tf_op jit(solution)/shard_map/ppermute | solution.py:163
  271.7 2.7 collective-permute-start.6
  274.5 1.2 constant_dynamic-update-slice_fusion.6
  275.7 1.1 constant_dynamic-update-slice_fusion.5
  276.7 1.0 constant_dynamic-update-slice_fusion.4
  277.8 1.0 constant_dynamic-update-slice_fusion.3
  278.8 2.3 constant_dynamic-update-slice_fusion.2
  281.1 2.3 constant_dynamic-update-slice_fusion.1
  283.4 95.5 %collective-permute-done.6 = bf16[2,1024,256]{2,1,0:T(8,128)(2,1)S(1)} collective-permute-done((bf16[2,1024,256]{2,1,0:T(8,128)(2,1)S(1)}, bf16[2,1024,256]{2,1,0:T(8,128)(2,1)S(1)}, u32[]{:S(2)}, u32[]{:S(2)}) %collective-permute-start.6) | collective-permute-done | bytes 1048608 | tf_op jit(solution)/shard_map/ppermute | solution.py:163
  378.9 1.0 constant_dynamic-update-slice_fusion.d_ref
  379.9 4.2 pad_maximum_fusion.h_ref
  384.2 1.3 copy-done.4
  385.6 16.2 %shard_map.95 = bf16[4096,256]{1,0:T(8,128)(2,1)S(1)} custom-call(s32[60]{0:T(128)S(1)} %pad_add_fusion.tile, s32[60]{0:T(128)S(1)} %pad_add_fusion.1.slot, s32[60]{0:T(128)S(1)} %pad_add_fusion.2.begin, s32[60]{0:T(128)S(1)} %pad_add_fusion.3.end, s32[60]{0:T(128)S(1)} %get-tuple-element.42.rank, f32[60]{0:T(128)S(1)} %get-tuple-element.41.scale, ...), custom_call_target="tpu_custom_call" | custom-call | flops 4026531840 | bytes 16777216 | tf_op jit(solution)/shard_map/pallas_call | solution.py:64
  402.1 2.8 collective-permute-done.18
  404.9 1.5 add_convert_fusion
  406.4 2.4 collective-permute-start.19
  408.8 1.5 collective-permute-start.21
  410.3 5.1 %collective-permute-done.19 = bf16[1024,128]{1,0:T(8,128)(2,1)S(1)} collective-permute-done((bf16[1024,128]{1,0:T(8,128)(2,1)S(1)}, bf16[1024,128]{1,0:T(8,128)(2,1)S(1)}, u32[]{:S(2)}, u32[]{:S(2)}) %collective-permute-start.19) | collective-permute-done | bytes 262176 | tf_op jit(solution)/shard_map/ppermute | solution.py:163
  415.4 2.6 collective-permute-done.20
  418.0 4.3 collective-permute-done.21
  422.5 1.5 collective-permute-done.22
  424.2 1.6 copy-done.3
  425.7 1.6 copy-done.5
  427.3 7.2 %shard_map.96 = (bf16[1024,512]{1,0:T(8,128)(2,1)}, bf16[1024,512]{1,0:T(8,128)(2,1)}) custom-call(s32[15]{0:T(128)S(1)} %subtract_select_fusion.tile, s32[15]{0:T(128)S(1)} %get-tuple-element.38.slot, s32[15]{0:T(128)S(1)} %fusion.23.begin, s32[15]{0:T(128)S(1)} %fusion.22.end, s32[15]{0:T(128)S(1)} %get-tuple-element.35.rank, ...), custom_call_target="tpu_custom_call" | custom-call | flops 503316480 | bytes 6291456 | tf_op jit(solution)/shard_map/pallas_call | solution.py:118
  (147 shorter events, 25.0 us)
Async XLA Ops:
  38.1 77.0 %collective-permute-start.10 = (bf16[1,2,128,512]{3,2,1,0:T(8,128)(2,1)}, bf16[1,2,128,512]{3,2,1,0:T(8,128)(2,1)}, u32[]{:S(2)}, u32[]{:S(2)}) collective-permute-start(bf16[1,2,128,512]{3,2,1,0:T(8,128)(2,1)} %get-tuple-element.79), channel_id=1, source_target_pairs={{0,2},{2,0},{4,6},{6,4},{8,10},{10,8},{12,14},{14,12},{1,3},{3,1},... | collective-permute-start | bytes 786440 | tf_op jit(solution)/shard_map/ppermute | solution.py:163
  39.8 75.8 %collective-permute-start.11 = (bf16[1,2,128,512]{3,2,1,0:T(8,128)(2,1)S(1)}, bf16[1,2,128,512]{3,2,1,0:T(8,128)(2,1)}, u32[]{:S(2)}, u32[]{:S(2)}) collective-permute-start(bf16[1,2,128,512]{3,2,1,0:T(8,128)(2,1)S(1)} %get-tuple-element.78), channel_id=1, source_target_pairs={{0,4},{2,6},{4,0},{6,2},{8,12},{10,14},{12,8},{14,10},{1,5},{3,7},... | collective-permute-start | bytes 786440 | tf_op jit(solution)/shard_map/ppermute | solution.py:163
  40.1 76.0 %collective-permute-start.12 = (bf16[1,2,128,512]{3,2,1,0:T(8,128)(2,1)S(1)}, bf16[1,2,128,512]{3,2,1,0:T(8,128)(2,1)}, u32[]{:S(2)}, u32[]{:S(2)}) collective-permute-start(bf16[1,2,128,512]{3,2,1,0:T(8,128)(2,1)S(1)} %get-tuple-element.77), channel_id=1, source_target_pairs={{0,6},{2,4},{4,2},{6,0},{8,14},{10,12},{12,10},{14,8},{1,7},{3,5},... | collective-permute-start | bytes 786440 | tf_op jit(solution)/shard_map/ppermute | solution.py:163
  41.6 77.1 %collective-permute-start.13 = (bf16[1,2,128,512]{3,2,1,0:T(8,128)(2,1)S(1)}, bf16[1,2,128,512]{3,2,1,0:T(8,128)(2,1)}, u32[]{:S(2)}, u32[]{:S(2)}) collective-permute-start(bf16[1,2,128,512]{3,2,1,0:T(8,128)(2,1)S(1)} %get-tuple-element.76), channel_id=1, source_target_pairs={{0,8},{2,10},{4,12},{6,14},{8,0},{10,2},{12,4},{14,6},{1,9},{3,11}... | collective-permute-start | bytes 786440 | tf_op jit(solution)/shard_map/ppermute | solution.py:163
  42.0 76.9 %collective-permute-start.14 = (bf16[1,2,128,512]{3,2,1,0:T(8,128)(2,1)S(1)}, bf16[1,2,128,512]{3,2,1,0:T(8,128)(2,1)}, u32[]{:S(2)}, u32[]{:S(2)}) collective-permute-start(bf16[1,2,128,512]{3,2,1,0:T(8,128)(2,1)S(1)} %get-tuple-element.75), channel_id=1, source_target_pairs={{0,10},{2,8},{4,14},{6,12},{8,2},{10,0},{12,6},{14,4},{1,11},{3,9}... | collective-permute-start | bytes 786440 | tf_op jit(solution)/shard_map/ppermute | solution.py:163
  58.0 17.1 %copy-start.22 = (s32[16]{0:T(128)S(1)}, s32[16]{0:T(128)}, u32[]{:S(2)}) copy-start(s32[16]{0:T(128)} %param.13) | copy-start | bytes 196
  58.0 17.1 %copy-start.23 = (s32[16]{0:T(128)S(1)}, s32[16]{0:T(128)}, u32[]{:S(2)}) copy-start(s32[16]{0:T(128)} %param.12) | copy-start | bytes 196
  79.8 26.0 %slice-start = ((s8[8388608]{0:T(1024)(128)(4,1)}), s8[4194304]{0:T(1024)(128)(4,1)S(1)}, s32[]{:S(2)}) async-start(s8[8388608]{0:T(1024)(128)(4,1)} %bitcast.192), calls=%async_computation | async-start | bytes 8388608
  79.8 26.0 %slice-start.1 = ((s8[8388608]{0:T(1024)(128)(4,1)}), s8[4194304]{0:T(1024)(128)(4,1)S(1)}, s32[]{:S(2)}) async-start(s8[8388608]{0:T(1024)(128)(4,1)} %bitcast.192), calls=%async_computation.1 | async-start | bytes 8388608
  105.8 4.7 %copy-start.6 = (bf16[2,4096,256]{2,1,0:T(8,128)(2,1)S(1)}, bf16[2,4096,256]{2,1,0:T(8,128)(2,1)}, u32[]{:S(2)}) copy-start(bf16[2,4096,256]{2,1,0:T(8,128)(2,1)} %reshape.827) | copy-start | bytes 12582916
  115.2 91.4 %collective-permute-start = (bf16[2,1024,256]{2,1,0:T(8,128)(2,1)}, bf16[2,1024,256]{2,1,0:T(8,128)(2,1)S(1)}, u32[]{:S(2)}, u32[]{:S(2)}) collective-permute-start(bf16[2,1024,256]{2,1,0:T(8,128)(2,1)} %get-tuple-element.67), channel_id=1, source_target_pairs={{0,2},{2,0},{4,6},{6,4},{8,10},{10,8},{12,14},{14,12},{1,3},{3,1},... | collective-permute-start | bytes 3145736 | tf_op jit(solution)/shard_map/ppermute | solution.py:163
  115.6 93.7 %collective-permute-start.1 = (bf16[2,1024,256]{2,1,0:T(8,128)(2,1)}, bf16[2,1024,256]{2,1,0:T(8,128)(2,1)S(1)}, u32[]{:S(2)}, u32[]{:S(2)}) collective-permute-start(bf16[2,1024,256]{2,1,0:T(8,128)(2,1)} %get-tuple-element.66), channel_id=1, source_target_pairs={{0,4},{2,6},{4,0},{6,2},{8,12},{10,14},{12,8},{14,10},{1,5},{3,7},... | collective-permute-start | bytes 3145736 | tf_op jit(solution)/shard_map/ppermute | solution.py:163
  116.1 96.2 %collective-permute-start.2 = (bf16[2,1024,256]{2,1,0:T(8,128)(2,1)}, bf16[2,1024,256]{2,1,0:T(8,128)(2,1)S(1)}, u32[]{:S(2)}, u32[]{:S(2)}) collective-permute-start(bf16[2,1024,256]{2,1,0:T(8,128)(2,1)} %get-tuple-element.65), channel_id=1, source_target_pairs={{0,6},{2,4},{4,2},{6,0},{8,14},{10,12},{12,10},{14,8},{1,7},{3,5},... | collective-permute-start | bytes 3145736 | tf_op jit(solution)/shard_map/ppermute | solution.py:163
  118.7 93.7 %collective-permute-start.3 = (bf16[2,1024,256]{2,1,0:T(8,128)(2,1)}, bf16[2,1024,256]{2,1,0:T(8,128)(2,1)S(1)}, u32[]{:S(2)}, u32[]{:S(2)}) collective-permute-start(bf16[2,1024,256]{2,1,0:T(8,128)(2,1)} %get-tuple-element.64), channel_id=1, source_target_pairs={{0,8},{2,10},{4,12},{6,14},{8,0},{10,2},{12,4},{14,6},{1,9},{3,11}... | collective-permute-start | bytes 3145736 | tf_op jit(solution)/shard_map/ppermute | solution.py:163
  118.9 74.0 %collective-permute-start.15 = (bf16[1,2,128,512]{3,2,1,0:T(8,128)(2,1)}, bf16[1,2,128,512]{3,2,1,0:T(8,128)(2,1)S(1)}, u32[]{:S(2)}, u32[]{:S(2)}) collective-permute-start(bf16[1,2,128,512]{3,2,1,0:T(8,128)(2,1)} %get-tuple-element.81), channel_id=1, source_target_pairs={{0,12},{2,14},{4,8},{6,10},{8,4},{10,6},{12,0},{14,2},{1,13},{3,15... | collective-permute-start | bytes 786440 | tf_op jit(solution)/shard_map/ppermute | solution.py:163
  192.9 21.1 %copy-start.18 = (bf16[1,2,128,512]{3,2,1,0:T(8,128)(2,1)}, bf16[1,2,128,512]{3,2,1,0:T(8,128)(2,1)S(1)}, u32[]{:S(2)}) copy-start(bf16[1,2,128,512]{3,2,1,0:T(8,128)(2,1)S(1)} %collective-permute-done.15) | copy-start | bytes 786436
  192.9 11.2 %collective-permute-start.16 = (bf16[1,2,128,512]{3,2,1,0:T(8,128)(2,1)S(1)}, bf16[1,2,128,512]{3,2,1,0:T(8,128)(2,1)S(1)}, u32[]{:S(2)}, u32[]{:S(2)}) collective-permute-start(bf16[1,2,128,512]{3,2,1,0:T(8,128)(2,1)S(1)} %get-tuple-element.74), channel_id=1, source_target_pairs={{0,14},{2,12},{4,10},{6,8},{8,6},{10,4},{12,2},{14,0},{1,15},{3,13... | collective-permute-start | bytes 786440 | tf_op jit(solution)/shard_map/ppermute | solution.py:163
  204.7 65.0 %collective-permute-start.4 = (bf16[2,1024,256]{2,1,0:T(8,128)(2,1)}, bf16[2,1024,256]{2,1,0:T(8,128)(2,1)}, u32[]{:S(2)}, u32[]{:S(2)}) collective-permute-start(bf16[2,1024,256]{2,1,0:T(8,128)(2,1)} %get-tuple-element.63), channel_id=1, source_target_pairs={{0,10},{2,8},{4,14},{6,12},{8,2},{10,0},{12,6},{14,4},{1,11},{3,9}... | collective-permute-start | bytes 3145736 | tf_op jit(solution)/shard_map/ppermute | solution.py:163
  206.5 5.9 %copy-start.10 = (bf16[2,1024,256]{2,1,0:T(8,128)(2,1)}, bf16[2,1024,256]{2,1,0:T(8,128)(2,1)S(1)}, u32[]{:S(2)}) copy-start(bf16[2,1024,256]{2,1,0:T(8,128)(2,1)S(1)} %collective-permute-done) | copy-start | bytes 3145732
  206.5 65.1 %collective-permute-start.5 = (bf16[2,1024,256]{2,1,0:T(8,128)(2,1)}, bf16[2,1024,256]{2,1,0:T(8,128)(2,1)}, u32[]{:S(2)}, u32[]{:S(2)}) collective-permute-start(bf16[2,1024,256]{2,1,0:T(8,128)(2,1)} %get-tuple-element.62), channel_id=1, source_target_pairs={{0,12},{2,14},{4,8},{6,10},{8,4},{10,6},{12,0},{14,2},{1,13},{3,15... | collective-permute-start | bytes 3145736 | tf_op jit(solution)/shard_map/ppermute | solution.py:163
  209.3 4.6 %copy-start.12 = (bf16[2,1024,256]{2,1,0:T(8,128)(2,1)}, bf16[2,1024,256]{2,1,0:T(8,128)(2,1)S(1)}, u32[]{:S(2)}) copy-start(bf16[2,1024,256]{2,1,0:T(8,128)(2,1)S(1)} %collective-permute-done.1) | copy-start | bytes 3145732
  209.3 170.6 %collective-permute-start.7 = (bf16[1024,1024]{1,0:T(8,128)(2,1)}, bf16[1024,1024]{1,0:T(8,128)(2,1)}, u32[]{:S(2)}, u32[]{:S(2)}) collective-permute-start(bf16[1024,1024]{1,0:T(8,128)(2,1)} %get-tuple-element.55), channel_id=1, source_target_pairs={{0,2},{2,0},{4,6},{6,4},{8,10},{10,8},{12,14},{14,12},{1,3},{3,1},... | collective-permute-start | bytes 6291464 | tf_op jit(solution)/shard_map/ppermute | solution.py:163
  212.3 1.6 copy-start.14
  212.3 167.6 %collective-permute-start.8 = (bf16[1024,1024]{1,0:T(8,128)(2,1)}, bf16[1024,1024]{1,0:T(8,128)(2,1)}, u32[]{:S(2)}, u32[]{:S(2)}) collective-permute-start(bf16[1024,1024]{1,0:T(8,128)(2,1)} %get-tuple-element.54), channel_id=1, source_target_pairs={{0,4},{2,6},{4,0},{6,2},{8,12},{10,14},{12,8},{14,10},{1,5},{3,7},... | collective-permute-start | bytes 6291464 | tf_op jit(solution)/shard_map/ppermute | solution.py:163
  212.4 1.5 copy-start.16
  212.4 167.5 %collective-permute-start.9 = (bf16[1024,1024]{1,0:T(8,128)(2,1)}, bf16[1024,1024]{1,0:T(8,128)(2,1)}, u32[]{:S(2)}, u32[]{:S(2)}) collective-permute-start(bf16[1024,1024]{1,0:T(8,128)(2,1)} %get-tuple-element.56), channel_id=1, source_target_pairs={{0,6},{2,4},{4,2},{6,0},{8,14},{10,12},{12,10},{14,8},{1,7},{3,5},... | collective-permute-start | bytes 6291464 | tf_op jit(solution)/shard_map/ppermute | solution.py:163
  214.1 60.3 %copy-start.19 = (bf16[1,2,128,512]{3,2,1,0:T(8,128)(2,1)S(1)}, bf16[1,2,128,512]{3,2,1,0:T(8,128)(2,1)}, u32[]{:S(2)}) copy-start(bf16[1,2,128,512]{3,2,1,0:T(8,128)(2,1)} %copy-done.18) | copy-start | bytes 786436
  214.1 55.6 %copy-start.8 = (bf16[1024,1024]{1,0:T(8,128)(2,1)S(1)}, bf16[1024,1024]{1,0:T(8,128)(2,1)}, u32[]{:S(2)}) copy-start(bf16[1024,1024]{1,0:T(8,128)(2,1)} %pad_maximum_fusion.2) | copy-start | bytes 6291460
  214.1 57.6 %copy-start.9 = (bf16[2,1024,256]{2,1,0:T(8,128)(2,1)S(1)}, bf16[2,1024,256]{2,1,0:T(8,128)(2,1)}, u32[]{:S(2)}) copy-start(bf16[2,1024,256]{2,1,0:T(8,128)(2,1)} %get-tuple-element.61) | copy-start | bytes 3145732
  214.1 60.4 %copy-start.21 = (bf16[1,2,128,512]{3,2,1,0:T(8,128)(2,1)S(1)}, bf16[1,2,128,512]{3,2,1,0:T(8,128)(2,1)}, u32[]{:S(2)}) copy-start(bf16[1,2,128,512]{3,2,1,0:T(8,128)(2,1)} %copy-done.20) | copy-start | bytes 786436
  214.1 60.4 %copy-start.11 = (bf16[2,1024,256]{2,1,0:T(8,128)(2,1)S(1)}, bf16[2,1024,256]{2,1,0:T(8,128)(2,1)}, u32[]{:S(2)}) copy-start(bf16[2,1024,256]{2,1,0:T(8,128)(2,1)} %copy-done.10) | copy-start | bytes 3145732
  214.2 61.5 %copy-start.13 = (bf16[2,1024,256]{2,1,0:T(8,128)(2,1)S(1)}, bf16[2,1024,256]{2,1,0:T(8,128)(2,1)}, u32[]{:S(2)}) copy-start(bf16[2,1024,256]{2,1,0:T(8,128)(2,1)} %copy-done.12) | copy-start | bytes 3145732
  217.1 59.6 %copy-start.15 = (bf16[2,1024,256]{2,1,0:T(8,128)(2,1)S(1)}, bf16[2,1024,256]{2,1,0:T(8,128)(2,1)}, u32[]{:S(2)}) copy-start(bf16[2,1024,256]{2,1,0:T(8,128)(2,1)} %copy-done.14) | copy-start | bytes 3145732
  220.1 57.6 %copy-start.17 = (bf16[2,1024,256]{2,1,0:T(8,128)(2,1)S(1)}, bf16[2,1024,256]{2,1,0:T(8,128)(2,1)}, u32[]{:S(2)}) copy-start(bf16[2,1024,256]{2,1,0:T(8,128)(2,1)} %copy-done.16) | copy-start | bytes 3145732
  269.7 114.5 %collective-permute-start.17 = (bf16[1024,1024]{1,0:T(8,128)(2,1)S(1)}, bf16[1024,1024]{1,0:T(8,128)(2,1)S(1)}, u32[]{:S(2)}, u32[]{:S(2)}) collective-permute-start(bf16[1024,1024]{1,0:T(8,128)(2,1)S(1)} %copy-done.8), channel_id=1, source_target_pairs={{0,1},{1,0},{2,3},{3,2},{4,5},{5,4},{6,7},{7,6},{8,9},{9,8},{10,11... | collective-permute-start | bytes 6291464 | tf_op jit(solution)/shard_map/ppermute | solution.py:166
  271.7 107.2 %collective-permute-start.6 = (bf16[2,1024,256]{2,1,0:T(8,128)(2,1)S(1)}, bf16[2,1024,256]{2,1,0:T(8,128)(2,1)S(1)}, u32[]{:S(2)}, u32[]{:S(2)}) collective-permute-start(bf16[2,1024,256]{2,1,0:T(8,128)(2,1)S(1)} %copy-done.9), channel_id=1, source_target_pairs={{0,14},{2,12},{4,10},{6,8},{8,6},{10,4},{12,2},{14,0},{1,15},{3,13... | collective-permute-start | bytes 3145736 | tf_op jit(solution)/shard_map/ppermute | solution.py:163
  274.4 4.4 %copy-start.2 = (bf16[8,2,128,512]{3,2,1,0:T(8,128)(2,1)}, bf16[8,2,128,512]{3,2,1,0:T(8,128)(2,1)S(1)}, u32[]{:S(2)}) copy-start(bf16[8,2,128,512]{3,2,1,0:T(8,128)(2,1)S(1)} %constant_dynamic-update-slice_fusion.7.u_ref) | copy-start | bytes 6291460
  277.8 102.2 %copy-start.7 = (bf16[1024,1024]{1,0:T(8,128)(2,1)S(1)}, bf16[1024,1024]{1,0:T(8,128)(2,1)}, u32[]{:S(2)}) copy-start(bf16[1024,1024]{1,0:T(8,128)(2,1)} %get-tuple-element.53) | copy-start | bytes 6291460
  379.9 5.7 %copy-start = (bf16[16,1024,256]{2,1,0:T(8,128)(2,1)S(1)}, bf16[16,1024,256]{2,1,0:T(8,128)(2,1)}, u32[]{:S(2)}) copy-start(bf16[16,1024,256]{2,1,0:T(8,128)(2,1)} %constant_dynamic-update-slice_fusion.d_ref) | copy-start | bytes 25165828
  384.2 1.3 copy-start.4
  402.0 2.9 collective-permute-start.18
  406.4 17.8 %copy-start.1 = (bf16[1024,1024]{1,0:T(8,128)(2,1)S(1)}, bf16[1024,1024]{1,0:T(8,128)(2,1)}, u32[]{:S(2)}) copy-start(bf16[1024,1024]{1,0:T(8,128)(2,1)} %pad_maximum_fusion.1.own_ref) | copy-start | bytes 6291460
  406.4 9.0 %collective-permute-start.19 = (bf16[1024,128]{1,0:T(8,128)(2,1)S(1)}, bf16[1024,128]{1,0:T(8,128)(2,1)S(1)}, u32[]{:S(2)}, u32[]{:S(2)}) collective-permute-start(bf16[1024,128]{1,0:T(8,128)(2,1)S(1)} %get-tuple-element.69), channel_id=1, source_target_pairs={{0,2},{2,0},{4,6},{6,4},{8,10},{10,8},{12,14},{14,12},{1,3},{3,1},... | collective-permute-start | bytes 786440 | tf_op jit(solution)/shard_map/ppermute | solution.py:163
  408.8 9.2 %collective-permute-start.20 = (bf16[1024,128]{1,0:T(8,128)(2,1)S(1)}, bf16[1024,128]{1,0:T(8,128)(2,1)S(1)}, u32[]{:S(2)}, u32[]{:S(2)}) collective-permute-start(bf16[1024,128]{1,0:T(8,128)(2,1)S(1)} %get-tuple-element.71), channel_id=1, source_target_pairs={{0,4},{2,6},{4,0},{6,2},{8,12},{10,14},{12,8},{14,10},{1,5},{3,7},... | collective-permute-start | bytes 786440 | tf_op jit(solution)/shard_map/ppermute | solution.py:163
  408.8 13.5 %collective-permute-start.21 = (bf16[1024,128]{1,0:T(8,128)(2,1)S(1)}, bf16[1024,128]{1,0:T(8,128)(2,1)S(1)}, u32[]{:S(2)}, u32[]{:S(2)}) collective-permute-start(bf16[1024,128]{1,0:T(8,128)(2,1)S(1)} %get-tuple-element.70), channel_id=1, source_target_pairs={{0,6},{2,4},{4,2},{6,0},{8,14},{10,12},{12,10},{14,8},{1,7},{3,5},... | collective-permute-start | bytes 786440 | tf_op jit(solution)/shard_map/ppermute | solution.py:163
  422.4 1.6 collective-permute-start.22
  424.1 1.6 copy-start.3
  425.7 1.6 copy-start.5
  (1 other events, 0.7 us)

commit v2 on v1

v2 whole, which is shorter than its diff:
```python
import functools

import jax
import jax.numpy as jnp
from jax import lax
from jax.experimental import pallas as pl
from jax.experimental.pallas import tpu as pltpu
from jax.sharding import PartitionSpec as P

TILE = 256
BF16 = jnp.bfloat16
F32 = jnp.float32


def table_lookup(indices, table):
    hit = indices[:, None] == jnp.arange(table.shape[0], dtype=jnp.int32)[None, :]
    return jnp.sum(jnp.where(hit, table[None, :], 0), axis=1)


def plan(lengths, ranks, rows):
    ends = jnp.cumsum(lengths)
    starts = ends - lengths
    top = jnp.arange(rows // TILE, dtype=jnp.int32) * TILE
    low = jnp.sum((ends[None, :] <= top[:, None]).astype(jnp.int32), axis=1)
    high = jnp.sum((starts[None, :] < top[:, None] + TILE).astype(jnp.int32), axis=1)
    return low, high, starts, ends, ranks, 1.0 / jnp.sqrt(ranks.astype(F32))


def shrink_kernel(tiles, count, low, high, begin, end, rank, scale, slot, h_ref, d_ref, o_ref):
    g = pl.program_id(0)
    top = g % tiles * TILE
    base = g // tiles * count
    shape = o_ref.shape
    half = shape[1] // 2
    o_ref[...] = jnp.zeros(shape, o_ref.dtype)

    @pl.loop(base + low[g], base + high[g])
    def _(j):
        grown = jnp.dot(h_ref[...], d_ref[slot[j]], preferred_element_type=F32) * scale[j]
        row = lax.broadcasted_iota(jnp.int32, shape, 0) + top
        col = lax.broadcasted_iota(jnp.int32, shape, 1)
        col = jnp.where(col >= half, col - half, col)
        mine = (row >= begin[j]) & (row < end[j])
        value = jnp.where(col < rank[j], grown, 0.0)
        o_ref[...] = jnp.where(mine, value, o_ref[...].astype(F32)).astype(o_ref.dtype)


def shrink_call(facts, slot, tokens, downs):
    rows, width = tokens.shape
    cols = downs.shape[2]
    sources, count = slot.shape
    tiles = rows // sources // TILE
    flat = [f.reshape(-1) for f in (*facts, slot)]
    return pl.pallas_call(
        functools.partial(shrink_kernel, tiles, count),
        grid_spec=pltpu.PrefetchScalarGridSpec(
            num_scalar_prefetch=7,
            grid=(sources * tiles,),
            in_specs=[
                pl.BlockSpec((TILE, width), lambda i, *_: (i, 0)),
                pl.BlockSpec(downs.shape, lambda i, *_: (0, 0, 0), pipeline_mode=pl.Buffered(1)),
            ],
            out_specs=pl.BlockSpec((TILE, cols), lambda i, *_: (i, 0)),
        ),
        out_shape=jax.ShapeDtypeStruct((rows, cols), BF16),
        compiler_params=pltpu.CompilerParams(
            dimension_semantics=("arbitrary",), vmem_limit_bytes=24 * 2**20
        ),
        cost_estimate=pl.CostEstimate(
            flops=4 * rows * width * cols, bytes_accessed=2 * rows * width * 2, transcendentals=0
        ),
    )(*flat, tokens, downs)


def grow_kernel(low, high, begin, end, slot, s_ref, u_ref, own_ref, other_ref, k_ref, v_ref):
    g = pl.program_id(0)
    half = s_ref.shape[1] // 2
    outs = (k_ref, v_ref)
    feat = k_ref.shape[1]
    row = lax.broadcasted_iota(jnp.int32, (TILE, feat), 0) + g * TILE
    for kv in range(2):
        cols = slice(kv * feat, (kv + 1) * feat)
        outs[kv][...] = jnp.zeros(k_ref.shape, BF16)

        @pl.loop(low[g], high[g])
        def _(j):
            grown = jnp.dot(s_ref[:, kv * half : (kv + 1) * half], u_ref[slot[j], kv], preferred_element_type=F32)
            grown = grown + (own_ref[:, cols].astype(F32) + other_ref[:, cols].astype(F32))
            mine = (row >= begin[j]) & (row < end[j])
            outs[kv][...] = jnp.where(mine, grown, outs[kv][...].astype(F32)).astype(BF16)


def grow_call(facts, slot, shrunk, ups, own, other):
    rows, cols = shrunk.shape
    feat = ups.shape[3]
    by_tile = lambda i, *_: (i, 0)
    return pl.pallas_call(
        grow_kernel,
        grid_spec=pltpu.PrefetchScalarGridSpec(
            num_scalar_prefetch=5,
            grid=(rows // TILE,),
            in_specs=[
                pl.BlockSpec((TILE, cols), by_tile),
                pl.BlockSpec(ups.shape, lambda i, *_: (0, 0, 0, 0), pipeline_mode=pl.Buffered(1)),
                pl.BlockSpec((TILE, 2 * feat), by_tile),
                pl.BlockSpec((TILE, 2 * feat), by_tile),
            ],
            out_specs=[pl.BlockSpec((TILE, feat), by_tile)] * 2,
        ),
        out_shape=[jax.ShapeDtypeStruct((rows, feat), BF16)] * 2,
        compiler_params=pltpu.CompilerParams(
            dimension_semantics=("arbitrary",), vmem_limit_bytes=24 * 2**20
        ),
        cost_estimate=pl.CostEstimate(
            flops=4 * rows * cols * feat, bytes_accessed=6 * rows * feat * 2, transcendentals=0
        ),
    )(*facts[:4], slot, shrunk, ups, own, other)


def per_device(
    replicas,
    cores,
    hidden_states,
    kv_weight,
    pool_down,
    pool_up,
    adapter_rank,
    pool_row,
    request_adapter,
    request_length,
):
    rows, width = hidden_states.shape
    kv_cols = kv_weight.shape[2]
    held, rank_max = pool_down.shape[0], pool_down.shape[3]
    team = 4 if replicas % 4 == 0 else 1
    part = width // team
    me = lax.axis_index("replica")
    core = lax.axis_index("tensor")

    def other_core(x):
        return lax.ppermute(x, "tensor", [(0, 1), (1, 0)])

    wanted = table_lookup(request_adapter[0], pool_row)
    count = request_length.shape[1]
    table = jnp.concatenate([wanted, request_length[0]])[None]
    table = lax.all_to_all(jnp.tile(table, (replicas, 1)), "replica", 0, 0, tiled=True)
    place = jnp.arange(pool_row.shape[0], dtype=jnp.int32)
    row_rank = jnp.sum(jnp.where(pool_row[None, :] == place[:, None], adapter_rank[None, :], 0), axis=1)

    def facts(o):
        line = lax.dynamic_slice_in_dim(table, me ^ o, 1, 0)[0]
        return line[:count], line[count:]

    teams = replicas // team

    def swap(x, o):
        return lax.ppermute(x, "replica", [(i, i ^ o) for i in range(replicas)])

    def share(o):
        return lax.dynamic_slice_in_dim(hidden_states, ((me ^ o) % team) * part, part, 1)

    sent = [share(o) for o in range(1, team)]
    pool_down, *sent = lax.optimization_barrier((pool_down, *sent))
    tokens = [share(0)] + [swap(x, o + 1) for o, x in enumerate(sent)]
    downs = pool_down.reshape(held, width, 2 * rank_max)
    downs = jnp.concatenate([downs[:, i * part : (i + 1) * part] for i in range(team)] * teams, axis=0)
    downs, table = lax.optimization_barrier((downs, table))
    down_all = lax.all_to_all(
        downs,
        "replica",
        0,
        0,
        tiled=True,
    )

    product = jnp.dot(
        hidden_states, kv_weight.reshape(width, 2 * kv_cols), preferred_element_type=F32
    ).astype(BF16)
    feat = kv_cols // cores
    if cores == 2:

        def features(c):
            return jnp.concatenate(
                [lax.dynamic_slice_in_dim(product, kv * kv_cols + c * feat, feat, 1) for kv in range(2)], axis=1
            )

        base_own = features(core)
        base_other = other_core(features(1 - core))
    else:
        base_own = jnp.concatenate(
            [
                lax.psum_scatter(
                    product[:, kv * kv_cols : (kv + 1) * kv_cols], "tensor", scatter_dimension=1, tiled=True
                )
                for kv in range(2)
            ],
            axis=1,
        )
        base_other = jnp.zeros_like(base_own)

    all_need = table[:, :count]
    asked = jnp.sum(jnp.where(all_need // held == me, all_need % held, 0), axis=1)
    down_all, base_own, base_other, pool_up = lax.optimization_barrier(
        (down_all, base_own, base_other, pool_up)
    )
    ups = lax.all_to_all(
        jnp.concatenate([lax.dynamic_slice_in_dim(pool_up, asked[i], 1, 0) for i in range(replicas)], axis=0),
        "replica",
        0,
        0,
        tiled=True,
    )

    plans, needs = [], []
    for o in range(team):
        need, lengths = facts(o)
        needs.append(need)
        plans.append(plan(lengths, table_lookup(need, row_rank), rows))
    partial = shrink_call(
        [jnp.stack(f) for f in zip(*plans)], jnp.stack(needs), jnp.concatenate(tokens, axis=0), down_all
    ).reshape(team, rows, 2 * rank_max)
    if cores == 2:
        keep = lax.dynamic_slice_in_dim(partial, core * rank_max, rank_max, 2)
        give = lax.dynamic_slice_in_dim(partial, (1 - core) * rank_max, rank_max, 2)
        partial = (keep.astype(F32) + other_core(give).astype(F32)).astype(BF16)
    else:
        partial = lax.psum(partial, "tensor")
    total = partial[0].astype(F32)
    for o in range(1, team):
        total = total + swap(partial[o], o).astype(F32)
    shrunk = total.astype(BF16)
    if cores == 2:
        peer = other_core(shrunk)
        shrunk = jnp.concatenate(
            [jnp.where(core == 0, shrunk, peer), jnp.where(core == 0, peer, shrunk)], axis=1
        )

    keys, values = grow_call(plans[0], needs[0] // held, shrunk, ups, base_own, base_other)
    return keys, values


def solution(mesh):
    placed = (
        P(("groups", "replica"), "tensor"),
        P("tensor", None, None),
        P(("groups", "replica"), "tensor", None, None),
        P(("groups", "replica"), None, None, "tensor"),
        P("groups"),
        P("groups"),
        P(("groups", "replica"), None),
        P(("groups", "replica"), None),
    )
    return jax.shard_map(
        functools.partial(per_device, mesh.shape["replica"], mesh.shape["tensor"]),
        mesh=mesh,
        in_specs=placed,
        out_specs=(P(("groups", "replica"), "tensor"), P(("groups", "replica"), "tensor")),
        check_vma=False,
    )
```

time: 436 us -> 347 us (0.80)
  waiting for transfers between devices: 235 us -> 167 us
  blocking collectives: 13.1 us -> 0 us
  other arithmetic: 25.9 us -> 14.7 us
  starting transfers between devices: 32.1 us -> 43.1 us
  local copies, waits for them, and re-layouts: 63.7 us -> 56.6 us
    ppermute x20 -> x6, waiting for transfers between devices: 231 us -> 48.3 us  [swap(): return lax.ppermute(x, 'replica', [(i, i ^ o) for i in range(replicas)])]
    all_to_all x0 -> x3, waiting for transfers between devices: none -> 114 us  [the longest x1 114 us: per_device(): down_all = lax.all_to_all(downs, 'replica', 0, 0, tiled=True)]
    all_to_all x0 -> x3, starting transfers between devices: none -> 35.5 us  [the longest x1 22.3 us: per_device(): lax.all_to_all(jnp.concatenate([lax.dynamic_slice_in_dim(pool_up, asked[i...]
    ppermute x20 -> x6, starting transfers between devices: 31.9 us -> 7.45 us  [swap(): return lax.ppermute(x, 'replica', [(i, i ^ o) for i in range(replicas)])]
    unnamed x1 -> x0, blocking collectives: 13.1 us -> none
    add x13 -> x1, other arithmetic: 5.86 us -> 0.01 us  [plan(): top[:, None] + TILE]
    dynamic_slice x3 -> x1, local copies, waits for them, and re-layouts: 10.4 us -> 6.94 us  [share(): lax.dynamic_slice_in_dim(hidden_states, (me ^ o) % team * part, part, 1)]
    unnamed x67 -> x29, local copies, waits for them, and re-layouts: 38.2 us -> 35 us
  transfers between devices with their start and end apart: 23 -> 12, of which waited for: 9 -> 7; matrix products, arithmetic and copies ran while one was open for 22% -> 26% of each run, Pallas kernels for 0% -> 5%
where the time goes in v2:
time: 347 us; the launch traced here: 346 us
  waiting for transfers between devices  167 us (48%)
  local copies, waits for them, and re-layouts  56.6 us (16%)
  starting transfers between devices  43.1 us (12%)
  Pallas kernels  26.6 us (8%)
  matrix products  22.7 us (7%)
  between operations  15.9 us (5%)
  other arithmetic  14.7 us (4%)
    all_to_all x1, waiting for transfers between devices, per_device(): down_all = lax.all_to_all(downs, 'replica', 0, 0, tiled=True)  114 us
    ppermute x6, waiting for transfers between devices, swap(): return lax.ppermute(x, 'replica', [(i, i ^ o) for i in range(replicas)])  48.3 us
    unnamed x29, local copies, waits for them, and re-layouts  35 us
    dot_general x1, matrix products, per_device(): jnp.dot(hidden_states, kv_weight.reshape(width, 2 * kv_cols), preferred_e...  22.7 us
    all_to_all x1, starting transfers between devices, per_device(): lax.all_to_all(jnp.concatenate([lax.dynamic_slice_in_dim(pool_up, asked[i...  22.3 us
    pallas_call x1, Pallas kernels, shrink_call(): pl.pallas_call(functools.partial(shrink_kernel, tiles, count), grid_spec=...  18.1 us
    pallas_call x1, Pallas kernels, grow_call(): pl.pallas_call(grow_kernel, grid_spec=pltpu.PrefetchScalarGridSpec(num_sc...  8.52 us
    reshape x1, local copies, waits for them, and re-layouts, per_device(): downs = pool_down.reshape(held, width, 2 * rank_max)  7.6 us
  transfers between devices with their start and end apart: 12, of which 7 were waited for; matrix products, arithmetic and copies ran while one was open for 26% of the time, Pallas kernels for 5%

profile of v2, /device:TPU:0, one launch (start us, length us, event | category | flops | bytes accessed | tf_op | source)
XLA Modules:
  0.0 346.3 jit_solution(16615231079090753913)
XLA Ops:
  0.6 0.9 select_reduce_fusion.5
  1.5 0.7 pad_add_fusion.6
  2.2 0.6 tile.2
  2.8 7.3 %all-to-all-start = ((s32[8,1,16]{2,1,0:T(1,128)}), s32[8,1,16]{2,1,0:T(1,128)S(1)}, u32[]{:S(2)}, u32[]{:S(2)}) async-start(s32[8,1,16]{2,1,0:T(1,128)} %tile.2), calls=%async_computation | async-start | bytes 8192 | tf_op jit(solution)/shard_map/all_to_all | solution.py:146
  10.1 6.9 %constant_dynamic-slice_fusion.5 = (bf16[1024,1024]{1,0:T(8,128)(2,1)}, bf16[1024,1024]{1,0:T(8,128)(2,1)}, bf16[1024,1024]{1,0:T(8,128)(2,1)}, bf16[1024,1024]{1,0:T(8,128)(2,1)}) fusion(bf16[1024,4096]{1,0:T(8,128)(2,1)} %param.8, s32[]{:T(128)S(6)} %select_n.156, s32[]{:T(128)S(6)} %select_n.142, s32[]{:T(128)S(6)} %select_n.140, s32[]{:T(128)S(6)} %select_n.138), kind=kLoop, calls=%fused_computation.44 | loop fusion | bytes 16777232 | tf_op jit(solution)/shard_map/dynamic_slice | solution.py:160
  17.0 7.6 %reshape.156 = bf16[2,4096,256]{2,1,0:T(8,128)(2,1)} reshape(bf16[2,4096,2,128]{3,2,1,0:T(2,128)(2,1)} %param.10) | data formatting | bytes 8388608 | tf_op jit(solution)/shard_map/reshape | solution.py:165
  24.6 2.5 slice_dynamic-update-slice_fusion.6
  27.1 2.3 slice_dynamic-update-slice_fusion.4
  29.4 2.3 slice_dynamic-update-slice_fusion.2
  31.7 1.0 slice_dynamic-update-slice_fusion
  32.7 1.1 slice_dynamic-update-slice_fusion.7
  33.8 1.0 slice_dynamic-update-slice_fusion.5
  34.8 1.0 slice_dynamic-update-slice_fusion.3
  35.9 1.1 slice_dynamic-update-slice_fusion.1
  37.0 6.0 %all-to-all-start.1 = ((bf16[16,1024,256]{2,1,0:T(8,128)(2,1)}), bf16[16,1024,256]{2,1,0:T(8,128)(2,1)}, u32[]{:S(2)}, u32[]{:S(2)}) async-start(bf16[16,1024,256]{2,1,0:T(8,128)(2,1)} %slice_dynamic-update-slice_fusion.1), calls=%async_computation.1 | async-start | bytes 16777216 | tf_op jit(solution)/shard_map/all_to_all | solution.py:168
  43.0 2.9 collective-permute-start.2
  45.9 0.6 collective-permute-start.1
  46.5 17.1 %copy.10 = bf16[512,8,2,1024]{3,1,2,0:T(8,128)(2,1)} copy(bf16[512,8,2,1024]{3,2,1,0:T(2,128)(2,1)} %bitcast.86) | data formatting | bytes 33554432
  63.6 22.7 %convolution_convert_fusion = bf16[1024,2048]{1,0:T(8,128)(2,1)S(1)} fusion(bf16[1024,4096]{1,0:T(8,128)(2,1)} %param.8, bf16[4096,2048]{1,0:T(8,128)(2,1)} %bitcast.87), kind=kOutput, calls=%fused_computation.1 | convolution fusion | flops 17181966336 | bytes 29360128 | tf_op jit(solution)/shard_map/dot_general | solution.py:176
  86.3 1.8 constant_dynamic-slice_fusion.2
  88.1 1.6 pad_maximum_fusion.2
  89.9 3.2 pad_maximum_fusion.1.own_ref
  94.7 0.7 fusion.8
  106.0 0.2 select_reduce_fusion.4
  111.6 114.1 %all-to-all-done.1.d_ref = bf16[16,1024,256]{2,1,0:T(8,128)(2,1)} async-done(((bf16[16,1024,256]{2,1,0:T(8,128)(2,1)}), bf16[16,1024,256]{2,1,0:T(8,128)(2,1)}, u32[]{:S(2)}, u32[]{:S(2)}) %all-to-all-start.1) | async-done | bytes 8388640 | tf_op jit(solution)/shard_map/all_to_all | solution.py:168
  225.7 0.7 dynamic-slice_dynamic-update-slice_fusion.7
  226.4 0.7 dynamic-slice_dynamic-update-slice_fusion.6
  227.1 0.7 dynamic-slice_dynamic-update-slice_fusion.5
  227.9 0.7 dynamic-slice_dynamic-update-slice_fusion.4
  228.6 0.7 dynamic-slice_dynamic-update-slice_fusion.3
  229.3 0.7 dynamic-slice_dynamic-update-slice_fusion.2
  230.0 0.7 dynamic-slice_dynamic-update-slice_fusion.1
  230.7 0.7 dynamic-slice_dynamic-update-slice_fusion
  231.5 22.3 %all-to-all-start.2 = ((bf16[8,2,128,512]{3,2,1,0:T(8,128)(2,1)}), bf16[8,2,128,512]{3,2,1,0:T(8,128)(2,1)}, u32[]{:S(2)}, u32[]{:S(2)}) async-start(bf16[8,2,128,512]{3,2,1,0:T(8,128)(2,1)} %dynamic-slice_dynamic-update-slice_fusion), calls=%async_computation.2 | async-start | bytes 4194304 | tf_op jit(solution)/shard_map/all_to_all | solution.py:206
  253.8 36.7 %collective-permute-done.1 = bf16[1024,1024]{1,0:T(8,128)(2,1)} collective-permute-done((bf16[1024,1024]{1,0:T(8,128)(2,1)}, bf16[1024,1024]{1,0:T(8,128)(2,1)}, u32[]{:S(2)}, u32[]{:S(2)}) %collective-permute-start.1) | collective-permute-done | bytes 2097184 | tf_op jit(solution)/shard_map/ppermute | solution.py:157
  290.5 4.5 %pad_maximum_fusion.h_ref = bf16[4096,1024]{1,0:T(8,128)(2,1)S(1)} fusion(bf16[1024,1024]{1,0:T(8,128)(2,1)} %collective-permute-done.2, bf16[1024,1024]{1,0:T(8,128)(2,1)} %collective-permute-done.1, bf16[1024,1024]{1,0:T(8,128)(2,1)} %collective-permute-done, bf16[1024,1024]{1,0:T(8,128)(2,1)} %get-tuple-element.34), kind=kLoop, calls=%fused_computation | loop fusion | flops 33554432 | bytes 16777216 | tf_op jit(solution)/shard_map/concatenate | solution.py:220
  295.0 18.1 %shard_map.95 = bf16[4096,256]{1,0:T(8,128)(2,1)S(1)} custom-call(s32[16]{0:T(128)S(1)} %reshape.162.low, s32[16]{0:T(128)S(1)} %reshape.166.high, s32[32]{0:T(128)S(1)} %reshape.167.begin, s32[32]{0:T(128)S(1)} %reshape.168.end, s32[32]{0:T(128)S(1)} %reshape.169.rank, f32[32]{0:T(128)S(1)} %reshape.170.scale, s32[32]{0:T(128)S(1)} %reshape.171.slot, ...), custom_call_target="tpu_custom_call" | custom-call | flops 4294967296 | bytes 16777216 | tf_op jit(solution)/shard_map/pallas_call | solution.py:54
  313.1 1.2 constant_dynamic-slice_fusion
  314.2 3.0 collective-permute-done.4
  317.2 1.5 add_convert_fusion
  318.8 3.3 collective-permute-start.7
  322.1 0.6 collective-permute-start.5
  322.8 6.5 %collective-permute-done.7 = bf16[1024,128]{1,0:T(8,128)(2,1)S(1)} collective-permute-done((bf16[1024,128]{1,0:T(8,128)(2,1)S(1)}, bf16[1024,128]{1,0:T(8,128)(2,1)S(1)}, u32[]{:S(2)}, u32[]{:S(2)}) %collective-permute-start.7) | collective-permute-done | bytes 262176 | tf_op jit(solution)/shard_map/ppermute | solution.py:157
  329.2 4.4 %collective-permute-done.6 = bf16[1024,128]{1,0:T(8,128)(2,1)S(1)} collective-permute-done((bf16[1024,128]{1,0:T(8,128)(2,1)S(1)}, bf16[1024,128]{1,0:T(8,128)(2,1)S(1)}, u32[]{:S(2)}, u32[]{:S(2)}) %collective-permute-start.6) | collective-permute-done | bytes 262176 | tf_op jit(solution)/shard_map/ppermute | solution.py:157
  333.6 0.7 collective-permute-done.5
  334.6 1.4 collective-permute-done.8
  336.2 1.6 copy-done.2
  337.8 8.5 %shard_map.96 = (bf16[1024,512]{1,0:T(8,128)(2,1)}, bf16[1024,512]{1,0:T(8,128)(2,1)}) custom-call(s32[4]{0:T(128)S(1)} %get-tuple-element.33.low, s32[4]{0:T(128)S(1)} %get-tuple-element.29.high, s32[8]{0:T(128)S(1)} %get-tuple-element.72.begin, s32[8]{0:T(128)S(1)} %bitcast.83, s32[8]{0:T(128)S(1)} %get-tuple-element.71.slot, ...), custom_call_target="tpu_custom_call" | custom-call | flops 536870912 | bytes 6291456 | tf_op jit(solution)/shard_map/pallas_call | solution.py:97
  (60 shorter events, 3.2 us)
Async XLA Ops:
  2.8 34.1 %all-to-all-start = ((s32[8,1,16]{2,1,0:T(1,128)}), s32[8,1,16]{2,1,0:T(1,128)S(1)}, u32[]{:S(2)}, u32[]{:S(2)}) async-start(s32[8,1,16]{2,1,0:T(1,128)} %tile.2), calls=%async_computation | async-start | bytes 8192 | tf_op jit(solution)/shard_map/all_to_all | solution.py:146
  24.6 7.0 %copy-start.3 = (bf16[2,4096,256]{2,1,0:T(8,128)(2,1)S(1)}, bf16[2,4096,256]{2,1,0:T(8,128)(2,1)}, u32[]{:S(2)}) copy-start(bf16[2,4096,256]{2,1,0:T(8,128)(2,1)} %reshape.156) | copy-start | bytes 12582916
  37.0 188.7 %all-to-all-start.1 = ((bf16[16,1024,256]{2,1,0:T(8,128)(2,1)}), bf16[16,1024,256]{2,1,0:T(8,128)(2,1)}, u32[]{:S(2)}, u32[]{:S(2)}) async-start(bf16[16,1024,256]{2,1,0:T(8,128)(2,1)} %slice_dynamic-update-slice_fusion.1), calls=%async_computation.1 | async-start | bytes 16777216 | tf_op jit(solution)/shard_map/all_to_all | solution.py:168
  43.0 210.8 %collective-permute-start.2 = (bf16[1024,1024]{1,0:T(8,128)(2,1)}, bf16[1024,1024]{1,0:T(8,128)(2,1)}, u32[]{:S(2)}, u32[]{:S(2)}) collective-permute-start(bf16[1024,1024]{1,0:T(8,128)(2,1)} %get-tuple-element.16), channel_id=1, source_target_pairs={{0,6},{2,4},{4,2},{6,0},{8,14},{10,12},{12,10},{14,8},{1,7},{3,5},... | collective-permute-start | bytes 6291464 | tf_op jit(solution)/shard_map/ppermute | solution.py:157
  45.9 244.6 %collective-permute-start.1 = (bf16[1024,1024]{1,0:T(8,128)(2,1)}, bf16[1024,1024]{1,0:T(8,128)(2,1)}, u32[]{:S(2)}, u32[]{:S(2)}) collective-permute-start(bf16[1024,1024]{1,0:T(8,128)(2,1)} %get-tuple-element.15), channel_id=1, source_target_pairs={{0,4},{2,6},{4,0},{6,2},{8,12},{10,14},{12,8},{14,10},{1,5},{3,7},... | collective-permute-start | bytes 6291464 | tf_op jit(solution)/shard_map/ppermute | solution.py:157
  46.4 244.1 %collective-permute-start = (bf16[1024,1024]{1,0:T(8,128)(2,1)}, bf16[1024,1024]{1,0:T(8,128)(2,1)}, u32[]{:S(2)}, u32[]{:S(2)}) collective-permute-start(bf16[1024,1024]{1,0:T(8,128)(2,1)} %get-tuple-element.14), channel_id=1, source_target_pairs={{0,2},{2,0},{4,6},{6,4},{8,10},{10,8},{12,14},{14,12},{1,3},{3,1},... | collective-permute-start | bytes 6291464 | tf_op jit(solution)/shard_map/ppermute | solution.py:157
  88.1 1.6 copy-start.5
  88.1 1.6 copy-start.6
  88.1 137.6 %copy-start.4 = (bf16[2,2,128,512]{3,2,1,0:T(8,128)(2,1)S(1)}, bf16[2,2,128,512]{3,2,1,0:T(8,128)(2,1)}, u32[]{:S(2)}) copy-start(bf16[2,2,128,512]{3,2,1,0:T(8,128)(2,1)} %param.11) | copy-start | bytes 1572868
  89.7 21.8 %collective-permute-start.3 = (bf16[1024,1024]{1,0:T(8,128)(2,1)}, bf16[1024,1024]{1,0:T(8,128)(2,1)S(1)}, u32[]{:S(2)}, u32[]{:S(2)}) collective-permute-start(bf16[1024,1024]{1,0:T(8,128)(2,1)} %pad_maximum_fusion.2), channel_id=1, source_target_pairs={{0,1},{1,0},{2,3},{3,2},{4,5},{5,4},{6,7},{7,6},{8,9},{9,8},{10,11... | collective-permute-start | bytes 6291464 | tf_op jit(solution)/shard_map/ppermute | solution.py:141
  111.5 119.9 %copy-start.1 = (bf16[1024,1024]{1,0:T(8,128)(2,1)}, bf16[1024,1024]{1,0:T(8,128)(2,1)S(1)}, u32[]{:S(2)}) copy-start(bf16[1024,1024]{1,0:T(8,128)(2,1)S(1)} %collective-permute-done.3.other_ref) | copy-start | bytes 6291460
  231.5 104.7 %all-to-all-start.2 = ((bf16[8,2,128,512]{3,2,1,0:T(8,128)(2,1)}), bf16[8,2,128,512]{3,2,1,0:T(8,128)(2,1)}, u32[]{:S(2)}, u32[]{:S(2)}) async-start(bf16[8,2,128,512]{3,2,1,0:T(8,128)(2,1)} %dynamic-slice_dynamic-update-slice_fusion), calls=%async_computation.2 | async-start | bytes 4194304 | tf_op jit(solution)/shard_map/all_to_all | solution.py:206
  314.2 3.0 collective-permute-start.4
  318.7 17.5 %copy-start = (bf16[1024,1024]{1,0:T(8,128)(2,1)S(1)}, bf16[1024,1024]{1,0:T(8,128)(2,1)}, u32[]{:S(2)}) copy-start(bf16[1024,1024]{1,0:T(8,128)(2,1)} %pad_maximum_fusion.1.own_ref) | copy-start | bytes 6291460
  318.8 10.4 %collective-permute-start.7 = (bf16[1024,128]{1,0:T(8,128)(2,1)S(1)}, bf16[1024,128]{1,0:T(8,128)(2,1)S(1)}, u32[]{:S(2)}, u32[]{:S(2)}) collective-permute-start(bf16[1024,128]{1,0:T(8,128)(2,1)S(1)} %get-tuple-element.43), channel_id=1, source_target_pairs={{0,6},{2,4},{4,2},{6,0},{8,14},{10,12},{12,10},{14,8},{1,7},{3,5},... | collective-permute-start | bytes 786440 | tf_op jit(solution)/shard_map/ppermute | solution.py:157
  322.1 11.5 %collective-permute-start.6 = (bf16[1024,128]{1,0:T(8,128)(2,1)S(1)}, bf16[1024,128]{1,0:T(8,128)(2,1)S(1)}, u32[]{:S(2)}, u32[]{:S(2)}) collective-permute-start(bf16[1024,128]{1,0:T(8,128)(2,1)S(1)} %get-tuple-element.44), channel_id=1, source_target_pairs={{0,4},{2,6},{4,0},{6,2},{8,12},{10,14},{12,8},{14,10},{1,5},{3,7},... | collective-permute-start | bytes 786440 | tf_op jit(solution)/shard_map/ppermute | solution.py:157
  322.1 12.2 %collective-permute-start.5 = (bf16[1024,128]{1,0:T(8,128)(2,1)S(1)}, bf16[1024,128]{1,0:T(8,128)(2,1)S(1)}, u32[]{:S(2)}, u32[]{:S(2)}) collective-permute-start(bf16[1024,128]{1,0:T(8,128)(2,1)S(1)} %get-tuple-element.42), channel_id=1, source_target_pairs={{0,2},{2,0},{4,6},{6,4},{8,10},{10,8},{12,14},{14,12},{1,3},{3,1},... | collective-permute-start | bytes 786440 | tf_op jit(solution)/shard_map/ppermute | solution.py:157
  334.5 1.6 collective-permute-start.8
  336.2 1.6 copy-start.2

commit v3 on v2

v3 whole, which is shorter than its diff:
```python
import functools

import jax
import jax.numpy as jnp
from jax import lax
from jax.experimental import pallas as pl
from jax.experimental.pallas import tpu as pltpu
from jax.sharding import PartitionSpec as P

TILE = 256
LOTS = 2
BF16 = jnp.bfloat16
F32 = jnp.float32


def table_lookup(indices, table):
    hit = indices[:, None] == jnp.arange(table.shape[0], dtype=jnp.int32)[None, :]
    return jnp.sum(jnp.where(hit, table[None, :], 0), axis=1)


def plan(lengths, ranks, rows):
    ends = jnp.cumsum(lengths)
    starts = ends - lengths
    top = jnp.arange(rows // TILE, dtype=jnp.int32) * TILE
    low = jnp.sum((ends[None, :] <= top[:, None]).astype(jnp.int32), axis=1)
    high = jnp.sum((starts[None, :] < top[:, None] + TILE).astype(jnp.int32), axis=1)
    return low, high, starts, ends, ranks, 1.0 / jnp.sqrt(ranks.astype(F32))


def shrink_kernel(first, low, high, begin, end, rank, scale, slot, column, h_ref, d_hbm, o_ref, d_ref, sems):
    g = pl.program_id(0)
    t = first + g
    top = t * TILE
    shape = o_ref.shape
    half = shape[1] // 2
    o_ref[...] = jnp.zeros(shape, o_ref.dtype)

    def fetch(j):
        return pltpu.make_async_copy(d_hbm.at[slot[j]], d_ref.at[j], sems.at[j])

    @pl.when(g == 0)
    def _():
        @pl.loop(low[first], high[first + pl.num_programs(0) - 1])
        def _(j):
            fetch(j).start()

    @pl.loop(low[t], high[t])
    def _(j):
        @pl.when((g == 0) | (begin[j] >= top))
        def _():
            fetch(j).wait()

        grown = jnp.dot(h_ref[...], d_ref[j], preferred_element_type=F32) * scale[j]
        row = lax.broadcasted_iota(jnp.int32, shape, 0) + top
        col = lax.broadcasted_iota(jnp.int32, shape, 1)
        col = jnp.where(col >= half, col - half, col)
        mine = (row >= begin[j]) & (row < end[j])
        value = jnp.where(col < rank[j], grown, 0.0)
        o_ref[...] = jnp.where(mine, value, o_ref[...].astype(F32)).astype(o_ref.dtype)


def shrink_call(facts, slot, first, tokens, column, downs):
    _, width, cols = downs.shape
    rows = tokens.shape[0]
    tiles = rows // TILE
    count = slot.shape[0]
    return pl.pallas_call(
        functools.partial(shrink_kernel, first),
        grid_spec=pltpu.PrefetchScalarGridSpec(
            num_scalar_prefetch=8,
            grid=(tiles,),
            in_specs=[
                pl.BlockSpec((TILE, width), lambda i, *refs: (i, refs[7][0])),
                pl.BlockSpec(memory_space=pl.ANY),
            ],
            out_specs=pl.BlockSpec((TILE, cols), lambda i, *_: (i, 0)),
            scratch_shapes=[
                pltpu.VMEM((count, width, cols), BF16),
                pltpu.SemaphoreType.DMA((count,)),
            ],
        ),
        out_shape=jax.ShapeDtypeStruct((rows, cols), BF16),
        compiler_params=pltpu.CompilerParams(
            dimension_semantics=("arbitrary",), vmem_limit_bytes=16 * 2**20
        ),
        cost_estimate=pl.CostEstimate(
            flops=4 * rows * width * cols, bytes_accessed=2 * rows * width * 2, transcendentals=0
        ),
    )(*facts, slot, column, tokens, downs)


def grow_kernel(first, low, high, begin, end, slot, s_ref, u_ref, own_ref, other_ref, *refs):
    k_ref, v_ref, wide = refs[-3:]
    t = first + pl.program_id(0)
    half = s_ref.shape[1] // 2
    outs = (k_ref, v_ref)
    feat = k_ref.shape[1]
    row = lax.broadcasted_iota(jnp.int32, (TILE, half), 0) + t * TILE
    wide[...] = jnp.zeros(wide.shape, BF16)

    @pl.loop(low[t], high[t])
    def _(j):
        mine = (row >= begin[j]) & (row < end[j])
        for kv in range(2):
            part = s_ref[:, kv * half : (kv + 1) * half].astype(F32)
            wide[kv, :, pl.ds(pl.multiple_of(slot[j] * half, half), half)] = jnp.where(mine, part, 0.0).astype(BF16)

    for kv in range(2):
        cols = slice(kv * feat, (kv + 1) * feat)
        ups = u_ref[:, kv].reshape(-1, feat)
        grown = jnp.dot(wide[kv], ups, preferred_element_type=F32)
        grown = grown + (own_ref[:, cols].astype(F32) + other_ref[:, cols].astype(F32))
        outs[kv][...] = grown.astype(BF16)


def grow_call(facts, slot, first, shrunk, ups, own, other, before):
    rows, cols = shrunk.shape
    feat = ups.shape[3]
    by_tile = lambda i, *_: (first + i, 0)
    return pl.pallas_call(
        functools.partial(grow_kernel, first),
        grid_spec=pltpu.PrefetchScalarGridSpec(
            num_scalar_prefetch=5,
            grid=(rows // TILE,),
            in_specs=[
                pl.BlockSpec((TILE, cols), lambda i, *_: (i, 0)),
                pl.BlockSpec(ups.shape, lambda i, *_: (0, 0, 0, 0), pipeline_mode=pl.Buffered(1)),
                pl.BlockSpec((TILE, 2 * feat), by_tile),
                pl.BlockSpec((TILE, 2 * feat), by_tile),
            ]
            + [pl.BlockSpec(memory_space=pl.ANY)] * len(before),
            out_specs=[pl.BlockSpec((TILE, feat), by_tile)] * 2,
            scratch_shapes=[pltpu.VMEM((2, TILE, ups.shape[0] * cols // 2), BF16)],
        ),
        out_shape=[jax.ShapeDtypeStruct((own.shape[0], feat), BF16)] * 2,
        input_output_aliases={9 + i: i for i in range(len(before))},
        compiler_params=pltpu.CompilerParams(
            dimension_semantics=("arbitrary",), vmem_limit_bytes=16 * 2**20
        ),
        cost_estimate=pl.CostEstimate(
            flops=4 * rows * cols * feat, bytes_accessed=6 * rows * feat * 2, transcendentals=0
        ),
    )(*facts[:4], slot, shrunk, ups, own, other, *before)


def send_kernel(pool_ref, o_ref):
    for t in range(o_ref.shape[0]):
        o_ref[t, 0, 0] = pool_ref[0]


def send_call(team, teams, pool_down):
    held, width, kinds, rank = pool_down.shape
    part = width // team
    return pl.pallas_call(
        send_kernel,
        grid=(team, held),
        in_specs=[pl.BlockSpec((1, part, kinds, rank), lambda i, a: (a, i, 0, 0))],
        out_specs=pl.BlockSpec((teams, 1, 1, part, kinds, rank), lambda i, a: (0, i, a, 0, 0, 0)),
        out_shape=jax.ShapeDtypeStruct((teams, team, held, part, kinds, rank), BF16),
        compiler_params=pltpu.CompilerParams(vmem_limit_bytes=32 * 2**20),
    )(pool_down).reshape(-1, part, kinds, rank)


def per_device(
    replicas,
    cores,
    hidden_states,
    kv_weight,
    pool_down,
    pool_up,
    adapter_rank,
    pool_row,
    request_adapter,
    request_length,
):
    rows, width = hidden_states.shape
    kv_cols = kv_weight.shape[2]
    held, rank_max = pool_down.shape[0], pool_down.shape[3]
    team = 4 if replicas % 4 == 0 else 1
    part = width // team
    me = lax.axis_index("replica")
    core = lax.axis_index("tensor")

    def other_core(x):
        return lax.ppermute(x, "tensor", [(0, 1), (1, 0)])

    wanted = table_lookup(request_adapter[0], pool_row)
    count = request_length.shape[1]
    table = jnp.concatenate([wanted, request_length[0]])[None]
    table = lax.all_to_all(jnp.tile(table, (replicas, 1)), "replica", 0, 0, tiled=True)
    place = jnp.arange(pool_row.shape[0], dtype=jnp.int32)
    row_rank = jnp.sum(jnp.where(pool_row[None, :] == place[:, None], adapter_rank[None, :], 0), axis=1)

    def facts(o):
        line = lax.dynamic_slice_in_dim(table, me ^ o, 1, 0)[0]
        return line[:count], line[count:]

    teams = replicas // team

    def swap(x, o):
        return lax.ppermute(x, "replica", [(i, i ^ o) for i in range(replicas)])

    lot = rows // LOTS

    def share(o, c):
        cut = lax.dynamic_slice(hidden_states, (c * lot, ((me ^ o) % team) * part), (lot, part))
        return swap(cut, o)

    early = [share(o, 0) for o in range(1, team)]
    downs = send_call(team, teams, pool_down)
    downs, table = lax.optimization_barrier((downs, table))
    down_all = lax.all_to_all(
        downs,
        "replica",
        0,
        0,
        tiled=True,
    )

    late = [[share(o, c) for o in range(1, team)] for c in range(1, LOTS)]

    product = jnp.dot(
        hidden_states, kv_weight.reshape(width, 2 * kv_cols), preferred_element_type=F32
    ).astype(BF16)
    feat = kv_cols // cores
    if cores == 2:

        def features(c):
            return jnp.concatenate(
                [lax.dynamic_slice_in_dim(product, kv * kv_cols + c * feat, feat, 1) for kv in range(2)], axis=1
            )

        base_own = features(core)
        base_other = other_core(features(1 - core))
    else:
        base_own = jnp.concatenate(
            [
                lax.psum_scatter(
                    product[:, kv * kv_cols : (kv + 1) * kv_cols], "tensor", scatter_dimension=1, tiled=True
                )
                for kv in range(2)
            ],
            axis=1,
        )
        base_other = jnp.zeros_like(base_own)

    all_need = table[:, :count]
    asked = jnp.sum(jnp.where(all_need // held == me, all_need % held, 0), axis=1)
    down_all, pool_up = lax.optimization_barrier((down_all, pool_up))
    early, base_own, base_other = lax.optimization_barrier((early, base_own, base_other))
    tokens = [early] + late
    down_all = down_all.reshape(-1, part, 2 * rank_max)
    ups = lax.all_to_all(
        jnp.concatenate([lax.dynamic_slice_in_dim(pool_up, asked[i], 1, 0) for i in range(replicas)], axis=0),
        "replica",
        0,
        0,
        tiled=True,
    )

    plans, needs = [], []
    for o in range(team):
        need, lengths = facts(o)
        needs.append(need)
        plans.append(plan(lengths, table_lookup(need, row_rank), rows))
    column = jnp.reshape(me % team, (1,)).astype(jnp.int32)
    zero = jnp.zeros((1,), jnp.int32)

    def over_cores(one):
        if cores != 2:
            return lax.psum(one, "tensor")
        keep = lax.dynamic_slice_in_dim(one, core * rank_max, rank_max, 1)
        give = lax.dynamic_slice_in_dim(one, (1 - core) * rank_max, rank_max, 1)
        return (keep.astype(F32) + other_core(give).astype(F32)).astype(BF16)

    own = over_cores(shrink_call(plans[0], needs[0], 0, hidden_states, column, down_all))
    out = ()
    per_lot = lot // TILE
    for c in range(LOTS):
        total = own[c * lot : (c + 1) * lot].astype(F32)
        for o in range(1, team):
            one = over_cores(shrink_call(plans[o], needs[o], c * per_lot, tokens[c][o - 1], zero, down_all))
            total = total + swap(one, o).astype(F32)
        shrunk = total.astype(BF16)
        if cores == 2:
            peer = other_core(shrunk)
            shrunk = jnp.concatenate(
                [jnp.where(core == 0, shrunk, peer), jnp.where(core == 0, peer, shrunk)], axis=1
            )
        out = grow_call(plans[0], needs[0] // held, c * per_lot, shrunk, ups, base_own, base_other, out)
    keys, values = out
    return keys, values


def solution(mesh):
    placed = (
        P(("groups", "replica"), "tensor"),
        P("tensor", None, None),
        P(("groups", "replica"), "tensor", None, None),
        P(("groups", "replica"), None, None, "tensor"),
        P("groups"),
        P("groups"),
        P(("groups", "replica"), None),
        P(("groups", "replica"), None),
    )
    return jax.shard_map(
        functools.partial(per_device, mesh.shape["replica"], mesh.shape["tensor"]),
        mesh=mesh,
        in_specs=placed,
        out_specs=(P(("groups", "replica"), "tensor"), P(("groups", "replica"), "tensor")),
        check_vma=False,
    )
```

time: 347 us -> 318 us (0.916); the launches traced: 346 us -> 312 us
  waiting for transfers between devices: 167 us -> 126 us
  Pallas kernels: 26.6 us -> 37.1 us
  local copies, waits for them, and re-layouts: 56.6 us -> 65.6 us
  starting transfers between devices: 43.1 us -> 36.5 us
  other arithmetic: 14.7 us -> 8.46 us
    all_to_all x1, waiting for transfers between devices: 114 us -> 0.66 us  [per_device(): down_all = lax.all_to_all(downs, 'replica', 0, 0, tiled=True)]
    ppermute x6 -> x12, waiting for transfers between devices: 48.3 us -> 124 us  [swap(): return lax.ppermute(x, 'replica', [(i, i ^ o) for i in range(replicas)])]
    all_to_all x1, starting transfers between devices: 22.3 us -> 6.28 us  [per_device(): lax.all_to_all(jnp.concatenate([lax.dynamic_slice_in_dim(pool_up, asked[i...]
    pallas_call x2 -> x10, Pallas kernels: 26.6 us -> 37.1 us  [the longest x7 26 us: shrink_call(): pl.pallas_call(functools.partial(shrink_kernel, first), grid_spec=pltpu.P...]
    ppermute x6 -> x12, starting transfers between devices: 7.45 us -> 14.7 us  [swap(): return lax.ppermute(x, 'replica', [(i, i ^ o) for i in range(replicas)])]
    unnamed x29 -> x30, local copies, waits for them, and re-layouts: 35 us -> 41 us
    reshape x9 -> x2, local copies, waits for them, and re-layouts: 8.24 us -> 14.1 us  [the longest x1 14 us: per_device(): down_all = down_all.reshape(-1, part, 2 * rank_max)]
    concatenate x1 -> x0, other arithmetic: 4.5 us -> none  [per_device(): jnp.concatenate(tokens, axis=0)]
  transfers between devices with their start and end apart: 12 -> 25, of which waited for: 7 -> 13; matrix products, arithmetic and copies ran while one was open for 26% -> 24% of each run, Pallas kernels for 5% -> 9%
where the time goes in v3:
time: 318 us; the launch traced here: 312 us
  waiting for transfers between devices  126 us (40%)
  local copies, waits for them, and re-layouts  65.6 us (21%)
  Pallas kernels  37.1 us (12%)
  starting transfers between devices  36.5 us (11%)
  matrix products  22.7 us (7%)
  between operations  16.2 us (5%)
  other arithmetic  8.46 us (3%)
    ppermute x12, waiting for transfers between devices, swap(): return lax.ppermute(x, 'replica', [(i, i ^ o) for i in range(replicas)])  124 us
    unnamed x30, local copies, waits for them, and re-layouts  41 us
    pallas_call x7, Pallas kernels, shrink_call(): pl.pallas_call(functools.partial(shrink_kernel, first), grid_spec=pltpu.P...  26 us
    dot_general x1, matrix products, per_device(): jnp.dot(hidden_states, kv_weight.reshape(width, 2 * kv_cols), preferred_e...  22.7 us
    ppermute x12, starting transfers between devices, swap(): return lax.ppermute(x, 'replica', [(i, i ^ o) for i in range(replicas)])  14.7 us
    reshape x1, local copies, waits for them, and re-layouts, per_device(): down_all = down_all.reshape(-1, part, 2 * rank_max)  14 us
    pallas_call x2, Pallas kernels, grow_call(): pl.pallas_call(functools.partial(grow_kernel, first), grid_spec=pltpu.Pre...  9.86 us
    all_to_all x1, starting transfers between devices, per_device(): lax.all_to_all(jnp.tile(table, (replicas, 1)), 'replica', 0, 0, tiled=True)  7.25 us
  transfers between devices with their start and end apart: 25, of which 13 were waited for; matrix products, arithmetic and copies ran while one was open for 24% of the time, Pallas kernels for 9%

profile of v3, /device:TPU:0, one launch (start us, length us, event | category | flops | bytes accessed | tf_op | source)
XLA Modules:
  0.0 312.2 jit_solution(3975565472087396088)
XLA Ops:
  0.6 0.9 select_reduce_fusion.5
  1.5 0.7 pad_add_fusion
  2.8 7.3 %all-to-all-start = ((s32[8,1,16]{2,1,0:T(1,128)}), s32[8,1,16]{2,1,0:T(1,128)S(1)}, u32[]{:S(2)}, u32[]{:S(2)}) async-start(s32[8,1,16]{2,1,0:T(1,128)} %tile.2), calls=%async_computation | async-start | bytes 8192 | tf_op jit(solution)/shard_map/all_to_all | solution.py:190
  10.1 2.2 copy-done.5
  12.3 1.2 shard_map.95
  13.5 3.2 %copy-done.3 = bf16[2,4,2,1024,2,128]{5,4,3,2,1,0:T(2,128)(2,1)} copy-done((bf16[2,4,2,1024,2,128]{5,4,3,2,1,0:T(2,128)(2,1)}, bf16[2,4,2,1024,2,128]{5,4,3,2,1,0:T(2,128)(2,1)S(1)}, u32[]{:S(2)}) %copy-start.3) | copy-done | bytes 8388632
  16.7 6.0 %all-to-all-start.1 = ((bf16[16,1024,2,128]{3,2,1,0:T(2,128)(2,1)}), bf16[16,1024,2,128]{3,2,1,0:T(2,128)(2,1)}, u32[]{:S(2)}, u32[]{:S(2)}) async-start(bf16[16,1024,2,128]{3,2,1,0:T(2,128)(2,1)} %bitcast.77), calls=%async_computation.1 | async-start | bytes 16777216 | tf_op jit(solution)/shard_map/all_to_all | solution.py:212
  22.7 5.6 %constant_dynamic-slice_fusion.7 = (bf16[512,1024]{1,0:T(8,128)(2,1)}, bf16[512,1024]{1,0:T(8,128)(2,1)}, bf16[512,1024]{1,0:T(8,128)(2,1)}, bf16[512,1024]{1,0:...) fusion(bf16[1024,4096]{1,0:T(8,128)(2,1)} %h_ref.1, s32[]{:T(128)S(6)} %select_n.184, ...), kind=kLoop, calls=%fused_computation.33 | loop fusion | bytes 12582924 | tf_op jit(solution)/shard_map/dynamic_slice | solution.py:206
  28.2 2.0 collective-permute-start.1
  30.3 2.0 collective-permute-start.12
  32.3 1.5 collective-permute-start.13
  33.8 17.1 %copy.12 = bf16[512,8,2,1024]{3,1,2,0:T(8,128)(2,1)} copy(bf16[512,8,2,1024]{3,2,1,0:T(2,128)(2,1)} %bitcast.91) | data formatting | bytes 33554432
  50.9 22.7 %convolution_convert_fusion = bf16[1024,2048]{1,0:T(8,128)(2,1)S(1)} fusion(bf16[1024,4096]{1,0:T(8,128)(2,1)} %h_ref.1, bf16[4096,2048]{1,0:T(8,128)(2,1)} %bitcast.92), kind=kOutput, calls=%fused_computation | convolution fusion | flops 17181966336 | bytes 29360128 | tf_op jit(solution)/shard_map/dot_general | solution.py:222
  73.5 1.9 constant_dynamic-slice_fusion.4
  75.4 1.6 pad_maximum_fusion.1
  77.1 1.8 pad_maximum_fusion.own_ref
  97.1 62.4 %collective-permute-done.11.h_ref = bf16[512,1024]{1,0:T(8,128)(2,1)} collective-permute-done((bf16[512,1024]{1,0:T(8,128)(2,1)}, bf16[512,1024]{1,0:T(8,128)(2,1)}, u32[]{:S(2)}, u32[]{:S(2)}) %collective-permute-start.11) | collective-permute-done | bytes 1048608 | tf_op jit(solution)/shard_map/ppermute | solution.py:201
  159.5 22.7 %collective-permute-done.12.h_ref = bf16[512,1024]{1,0:T(8,128)(2,1)} collective-permute-done((bf16[512,1024]{1,0:T(8,128)(2,1)}, bf16[512,1024]{1,0:T(8,128)(2,1)}, u32[]{:S(2)}, u32[]{:S(2)}) %collective-permute-start.12) | collective-permute-done | bytes 1048608 | tf_op jit(solution)/shard_map/ppermute | solution.py:201
  182.3 3.7 %collective-permute-start.7 = (bf16[512,1024]{1,0:T(8,128)(2,1)}, bf16[512,1024]{1,0:T(8,128)(2,1)}, u32[]{:S(2)}, u32[]{:S(2)}) collective-permute-start(bf16[512,1024]{1,0:T(8,128)(2,1)} %get-tuple-element.39), channel_id=1, source_target_pairs={{0,6},{2,4},{4,2},{6,0},{8,14},{10,12},{12,10},{14,8},{1,7},{3,5},... | collective-permute-start | bytes 3145736 | tf_op jit(solution)/shard_map/ppermute | solution.py:201
  186.0 18.7 %collective-permute-done.13.h_ref = bf16[512,1024]{1,0:T(8,128)(2,1)S(1)} collective-permute-done((bf16[512,1024]{1,0:T(8,128)(2,1)}, bf16[512,1024]{1,0:T(8,128)(2,1)S(1)}, u32[]{:S(2)}, u32[]{:S(2)}) %collective-permute-start.13) | collective-permute-done | bytes 1048608 | tf_op jit(solution)/shard_map/ppermute | solution.py:201
  205.4 14.0 %reshape.96.d_hbm = bf16[16,1024,256]{2,1,0:T(8,128)(2,1)} reshape(bf16[16,1024,2,128]{3,2,1,0:T(2,128)(2,1)} %all-to-all-done.1) | data formatting | bytes 16777216 | tf_op jit(solution)/shard_map/reshape | solution.py:252
  219.4 3.4 %copy-done = bf16[16,1024,256]{2,1,0:T(8,128)(2,1)S(1)} copy-done((bf16[16,1024,256]{2,1,0:T(8,128)(2,1)S(1)}, bf16[16,1024,256]{2,1,0:T(8,128)(2,1)}, u32[]{:S(2)}) %copy-start) | copy-done | bytes 8388632
  222.8 3.8 %shard_map.97 = bf16[512,256]{1,0:T(8,128)(2,1)S(1)} custom-call(s32[4]{0:T(128)S(1)} %get-tuple-element.77.low, s32[4]{0:T(128)S(1)} %get-tuple-element.28.high, s32[8]{0:T(128)S(1)} %bitcast_subtract_fusion.4.begin, s32[8]{0:T(128)S(1)} %bitcast.89, s32[8]{0:T(128)S(1)} %get-tuple-element.25.rank, f32[8]{0:T(128)S(1)} %convert_rsqrt_fusion.2.scale, ...), custom_call_target="tpu_custom_call" | custom-call | flops 536870912 | bytes 2097152 | tf_op jit(solution)/shard_map/pallas_call | solution.py:67
  228.1 0.7 dynamic-slice_dynamic-update-slice_fusion.6
  228.8 0.7 dynamic-slice_dynamic-update-slice_fusion.5
  233.1 6.3 %all-to-all-start.2 = ((bf16[8,2,128,512]{3,2,1,0:T(8,128)(2,1)}), bf16[8,2,128,512]{3,2,1,0:T(8,128)(2,1)}, u32[]{:S(2)}, u32[]{:S(2)}) async-start(bf16[8,2,128,512]{3,2,1,0:T(8,128)(2,1)} %dynamic-slice_dynamic-update-slice_fusion), calls=%async_computation.2 | async-start | bytes 4194304 | tf_op jit(solution)/shard_map/all_to_all | solution.py:253
  239.4 3.4 %copy-done.1 = bf16[16,1024,256]{2,1,0:T(8,128)(2,1)S(1)} copy-done((bf16[16,1024,256]{2,1,0:T(8,128)(2,1)S(1)}, bf16[16,1024,256]{2,1,0:T(8,128)(2,1)}, u32[]{:S(2)}) %copy-start.1) | copy-done | bytes 8388632
  242.8 3.8 %shard_map.98 = bf16[512,256]{1,0:T(8,128)(2,1)S(1)} custom-call(s32[4]{0:T(128)S(1)} %get-tuple-element.76.low, s32[4]{0:T(128)S(1)} %get-tuple-element.29.high, s32[8]{0:T(128)S(1)} %bitcast_subtract_fusion.2.begin, s32[8]{0:T(128)S(1)} %bitcast.86, s32[8]{0:T(128)S(1)} %get-tuple-element.26.rank, f32[8]{0:T(128)S(1)} %convert_rsqrt_fusion.1.scale, ...), custom_call_target="tpu_custom_call" | custom-call | flops 536870912 | bytes 2097152 | tf_op jit(solution)/shard_map/pallas_call | solution.py:67
  246.9 10.1 %collective-permute-done.7.h_ref = bf16[512,1024]{1,0:T(8,128)(2,1)} collective-permute-done((bf16[512,1024]{1,0:T(8,128)(2,1)}, bf16[512,1024]{1,0:T(8,128)(2,1)}, u32[]{:S(2)}, u32[]{:S(2)}) %collective-permute-start.7) | collective-permute-done | bytes 1048608 | tf_op jit(solution)/shard_map/ppermute | solution.py:201
  257.0 3.4 %copy-done.2 = bf16[16,1024,256]{2,1,0:T(8,128)(2,1)S(1)} copy-done((bf16[16,1024,256]{2,1,0:T(8,128)(2,1)S(1)}, bf16[16,1024,256]{2,1,0:T(8,128)(2,1)}, u32[]{:S(2)}) %copy-start.2) | copy-done | bytes 8388632
  260.4 2.7 shard_map.99
  263.2 3.4 %copy-done.4 = bf16[1024,4096]{1,0:T(8,128)(2,1)S(1)} copy-done((bf16[1024,4096]{1,0:T(8,128)(2,1)S(1)}, bf16[1024,4096]{1,0:T(8,128)(2,1)}, u32[]{:S(2)}) %copy-start.4) | copy-done | bytes 8388632
  266.6 4.7 %shard_map.96 = bf16[1024,256]{1,0:T(8,128)(2,1)S(1)} custom-call(s32[4]{0:T(128)S(1)} %get-tuple-element.74.low, s32[4]{0:T(128)S(1)} %get-tuple-element.31.high, s32[8]{0:T(128)S(1)} %get-tuple-element.73.begin, s32[8]{0:T(128)S(1)} %bitcast.79, s32[8]{0:T(128)S(1)} %get-tuple-element.24.rank, f32[8]{0:T(128)S(1)} %convert_rsqrt_fusion.3.scale, ...), custom_call_target="tpu_custom_call" | custom-call | flops 1073741824 | bytes 4194304 | tf_op jit(solution)/shard_map/pallas_call | solution.py:67
  271.9 3.5 %shard_map.100 = bf16[512,256]{1,0:T(8,128)(2,1)S(1)} custom-call(s32[4]{0:T(128)S(1)} %get-tuple-element.77.low, s32[4]{0:T(128)S(1)} %get-tuple-element.28.high, s32[8]{0:T(128)S(1)} %bitcast_subtract_fusion.4.begin, s32[8]{0:T(128)S(1)} %bitcast.90, s32[8]{0:T(128)S(1)} %get-tuple-element.25.rank, f32[8]{0:T(128)S(1)} %convert_rsqrt_fusion.2.scale, ...), custom_call_target="tpu_custom_call" | custom-call | flops 536870912 | bytes 2097152 | tf_op jit(solution)/shard_map/pallas_call | solution.py:67
  275.5 3.8 %shard_map.101 = bf16[512,256]{1,0:T(8,128)(2,1)S(1)} custom-call(s32[4]{0:T(128)S(1)} %get-tuple-element.76.low, s32[4]{0:T(128)S(1)} %get-tuple-element.29.high, s32[8]{0:T(128)S(1)} %bitcast_subtract_fusion.2.begin, s32[8]{0:T(128)S(1)} %bitcast.87, s32[8]{0:T(128)S(1)} %get-tuple-element.26.rank, f32[8]{0:T(128)S(1)} %convert_rsqrt_fusion.1.scale, ...), custom_call_target="tpu_custom_call" | custom-call | flops 536870912 | bytes 2097152 | tf_op jit(solution)/shard_map/pallas_call | solution.py:67
  279.4 3.6 %shard_map.102 = bf16[512,256]{1,0:T(8,128)(2,1)S(1)} custom-call(s32[4]{0:T(128)S(1)} %get-tuple-element.75.low, s32[4]{0:T(128)S(1)} %get-tuple-element.30.high, s32[8]{0:T(128)S(1)} %bitcast_subtract_fusion.begin, s32[8]{0:T(128)S(1)} %bitcast.84, s32[8]{0:T(128)S(1)} %get-tuple-element.27.rank, f32[8]{0:T(128)S(1)} %convert_rsqrt_fusion.scale, ...), custom_call_target="tpu_custom_call" | custom-call | flops 536870912 | bytes 2097152 | tf_op jit(solution)/shard_map/pallas_call | solution.py:67
  283.6 0.9 add_convert_fusion.8
  285.6 2.9 collective-permute-start.9
  288.6 2.0 collective-permute-done.3
  290.6 1.7 collective-permute-start.20
  292.4 1.6 collective-permute-done.6
  294.1 1.4 collective-permute-done.9
  295.5 0.9 collective-permute-done.16
  296.4 3.3 %collective-permute-done.18 = bf16[512,128]{1,0:T(8,128)(2,1)S(1)} collective-permute-done((bf16[512,128]{1,0:T(8,128)(2,1)S(1)}, bf16[512,128]{1,0:T(8,128)(2,1)S(1)}, u32[]{:S(2)}, u32[]{:S(2)}) %collective-permute-start.18) | collective-permute-done | bytes 131104 | tf_op jit(solution)/shard_map/ppermute | solution.py:201
  299.7 0.8 collective-permute-done.20
  301.2 0.8 collective-permute-done.21
  302.3 5.1 %shard_map.103 = (bf16[1024,512]{1,0:T(8,128)(2,1)}, bf16[1024,512]{1,0:T(8,128)(2,1)}) custom-call(s32[4]{0:T(128)S(1)} %get-tuple-element.74.low, s32[4]{0:T(128)S(1)} %get-tuple-element.31.high, s32[8]{0:T(128)S(1)} %get-tuple-element.73.begin, s32[8]{0:T(128)S(1)} %bitcast.80, s32[8]{0:T(128)S(1)} %get-tuple-element.72.slot, ...), custom_call_target="tpu_custom_call" | custom-call | flops 268435456 | bytes 3145728 | tf_op jit(solution)/shard_map/pallas_call | solution.py:120
  307.4 4.8 %shard_map.104 = (bf16[1024,512]{1,0:T(8,128)(2,1)}, bf16[1024,512]{1,0:T(8,128)(2,1)}) custom-call(s32[4]{0:T(128)S(1)} %get-tuple-element.74.low, s32[4]{0:T(128)S(1)} %get-tuple-element.31.high, s32[8]{0:T(128)S(1)} %get-tuple-element.73.begin, s32[8]{0:T(128)S(1)} %bitcast.81, ...), custom_call_target="tpu_custom_call", output_to_operand_aliasing={{0}: (9, {}), {1}: (10, {})} | custom-call | flops 268435456 | bytes 3145728 | tf_op jit(solution)/shard_map/pallas_call | solution.py:120
  (100 shorter events, 13.2 us)
Async XLA Ops:
  2.8 13.9 %all-to-all-start = ((s32[8,1,16]{2,1,0:T(1,128)}), s32[8,1,16]{2,1,0:T(1,128)S(1)}, u32[]{:S(2)}, u32[]{:S(2)}) async-start(s32[8,1,16]{2,1,0:T(1,128)} %tile.2), calls=%async_computation | async-start | bytes 8192 | tf_op jit(solution)/shard_map/all_to_all | solution.py:190
  10.1 2.2 copy-start.5
  13.5 3.2 %copy-start.3 = (bf16[2,4,2,1024,2,128]{5,4,3,2,1,0:T(2,128)(2,1)}, bf16[2,4,2,1024,2,128]{5,4,3,2,1,0:T(2,128)(2,1)S(1)}, u32[]{:S(2)}) copy-start(bf16[2,4,2,1024,2,128]{5,4,3,2,1,0:T(2,128)(2,1)S(1)} %shard_map.95) | copy-start | bytes 25165828
  16.7 188.7 %all-to-all-start.1 = ((bf16[16,1024,2,128]{3,2,1,0:T(2,128)(2,1)}), bf16[16,1024,2,128]{3,2,1,0:T(2,128)(2,1)}, u32[]{:S(2)}, u32[]{:S(2)}) async-start(bf16[16,1024,2,128]{3,2,1,0:T(2,128)(2,1)} %bitcast.77), calls=%async_computation.1 | async-start | bytes 16777216 | tf_op jit(solution)/shard_map/all_to_all | solution.py:212
  28.2 191.2 %collective-permute-start.1 = (bf16[512,1024]{1,0:T(8,128)(2,1)}, bf16[512,1024]{1,0:T(8,128)(2,1)}, u32[]{:S(2)}, u32[]{:S(2)}) collective-permute-start(bf16[512,1024]{1,0:T(8,128)(2,1)} %get-tuple-element.41), channel_id=1, source_target_pairs={{0,2},{2,0},{4,6},{6,4},{8,10},{10,8},{12,14},{14,12},{1,3},{3,1},... | collective-permute-start | bytes 3145736 | tf_op jit(solution)/shard_map/ppermute | solution.py:201
  30.3 129.3 %collective-permute-start.11 = (bf16[512,1024]{1,0:T(8,128)(2,1)}, bf16[512,1024]{1,0:T(8,128)(2,1)}, u32[]{:S(2)}, u32[]{:S(2)}) collective-permute-start(bf16[512,1024]{1,0:T(8,128)(2,1)} %get-tuple-element.38), channel_id=1, source_target_pairs={{0,2},{2,0},{4,6},{6,4},{8,10},{10,8},{12,14},{14,12},{1,3},{3,1},... | collective-permute-start | bytes 3145736 | tf_op jit(solution)/shard_map/ppermute | solution.py:201
  30.3 152.0 %collective-permute-start.12 = (bf16[512,1024]{1,0:T(8,128)(2,1)}, bf16[512,1024]{1,0:T(8,128)(2,1)}, u32[]{:S(2)}, u32[]{:S(2)}) collective-permute-start(bf16[512,1024]{1,0:T(8,128)(2,1)} %get-tuple-element.37), channel_id=1, source_target_pairs={{0,4},{2,6},{4,0},{6,2},{8,12},{10,14},{12,8},{14,10},{1,5},{3,7},... | collective-permute-start | bytes 3145736 | tf_op jit(solution)/shard_map/ppermute | solution.py:201
  32.3 172.4 %collective-permute-start.13 = (bf16[512,1024]{1,0:T(8,128)(2,1)}, bf16[512,1024]{1,0:T(8,128)(2,1)S(1)}, u32[]{:S(2)}, u32[]{:S(2)}) collective-permute-start(bf16[512,1024]{1,0:T(8,128)(2,1)} %get-tuple-element.36), channel_id=1, source_target_pairs={{0,6},{2,4},{4,2},{6,0},{8,14},{10,12},{12,10},{14,8},{1,7},{3,5},... | collective-permute-start | bytes 3145736 | tf_op jit(solution)/shard_map/ppermute | solution.py:201
  75.4 1.6 copy-start.7
  75.4 1.6 copy-start.8
  77.0 127.8 %collective-permute-start.14 = (bf16[1024,1024]{1,0:T(8,128)(2,1)}, bf16[1024,1024]{1,0:T(8,128)(2,1)}, u32[]{:S(2)}, u32[]{:S(2)}) collective-permute-start(bf16[1024,1024]{1,0:T(8,128)(2,1)} %pad_maximum_fusion.1), channel_id=1, source_target_pairs={{0,1},{1,0},{2,3},{3,2},{4,5},{5,4},{6,7},{7,6},{8,9},{9,8},{10,11... | collective-permute-start | bytes 6291464 | tf_op jit(solution)/shard_map/ppermute | solution.py:185
  159.5 79.9 %collective-permute-start.4 = (bf16[512,1024]{1,0:T(8,128)(2,1)}, bf16[512,1024]{1,0:T(8,128)(2,1)}, u32[]{:S(2)}, u32[]{:S(2)}) collective-permute-start(bf16[512,1024]{1,0:T(8,128)(2,1)} %get-tuple-element.40), channel_id=1, source_target_pairs={{0,4},{2,6},{4,0},{6,2},{8,12},{10,14},{12,8},{14,10},{1,5},{3,7},... | collective-permute-start | bytes 3145736 | tf_op jit(solution)/shard_map/ppermute | solution.py:201
  182.3 74.7 %collective-permute-start.7 = (bf16[512,1024]{1,0:T(8,128)(2,1)}, bf16[512,1024]{1,0:T(8,128)(2,1)}, u32[]{:S(2)}, u32[]{:S(2)}) collective-permute-start(bf16[512,1024]{1,0:T(8,128)(2,1)} %get-tuple-element.39), channel_id=1, source_target_pairs={{0,6},{2,4},{4,2},{6,0},{8,14},{10,12},{12,10},{14,8},{1,7},{3,5},... | collective-permute-start | bytes 3145736 | tf_op jit(solution)/shard_map/ppermute | solution.py:201
  219.4 3.4 %copy-start = (bf16[16,1024,256]{2,1,0:T(8,128)(2,1)S(1)}, bf16[16,1024,256]{2,1,0:T(8,128)(2,1)}, u32[]{:S(2)}) copy-start(bf16[16,1024,256]{2,1,0:T(8,128)(2,1)} %reshape.96.d_hbm) | copy-start | bytes 25165828
  222.8 4.5 %copy-start.6 = (bf16[2,2,128,512]{3,2,1,0:T(8,128)(2,1)S(1)}, bf16[2,2,128,512]{3,2,1,0:T(8,128)(2,1)}, u32[]{:S(2)}) copy-start(bf16[2,2,128,512]{3,2,1,0:T(8,128)(2,1)} %param.11) | copy-start | bytes 1572868
  227.4 55.7 %collective-permute-start.2 = (bf16[512,128]{1,0:T(8,128)(2,1)}, bf16[512,128]{1,0:T(8,128)(2,1)}, u32[]{:S(2)}, u32[]{:S(2)}) collective-permute-start(bf16[512,128]{1,0:T(8,128)(2,1)} %constant_dynamic-slice_fusion.14), channel_id=1, source_target_pairs={{0,1},{1,0},{2,3},{3,2},{4,5},{5,4},{6,7},{7,6},{8,9},{9,8},{10,11... | collective-permute-start | bytes 393224 | tf_op jit(solution)/shard_map/ppermute | solution.py:185
  233.1 69.2 %all-to-all-start.2 = ((bf16[8,2,128,512]{3,2,1,0:T(8,128)(2,1)}), bf16[8,2,128,512]{3,2,1,0:T(8,128)(2,1)}, u32[]{:S(2)}, u32[]{:S(2)}) async-start(bf16[8,2,128,512]{3,2,1,0:T(8,128)(2,1)} %dynamic-slice_dynamic-update-slice_fusion), calls=%async_computation.2 | async-start | bytes 4194304 | tf_op jit(solution)/shard_map/all_to_all | solution.py:253
  239.4 3.4 %copy-start.1 = (bf16[16,1024,256]{2,1,0:T(8,128)(2,1)S(1)}, bf16[16,1024,256]{2,1,0:T(8,128)(2,1)}, u32[]{:S(2)}) copy-start(bf16[16,1024,256]{2,1,0:T(8,128)(2,1)} %reshape.96.d_hbm) | copy-start | bytes 25165828
  242.8 20.4 %slice-start = ((s8[8388608]{0:T(1024)(128)(4,1)}), s8[4194304]{0:T(1024)(128)(4,1)S(1)}, s32[]{:S(2)}) async-start(s8[8388608]{0:T(1024)(128)(4,1)} %bitcast.75), calls=%async_computation.3 | async-start | bytes 8388608
  246.6 37.9 %collective-permute-start.5 = (bf16[512,128]{1,0:T(8,128)(2,1)S(1)}, bf16[512,128]{1,0:T(8,128)(2,1)S(1)}, u32[]{:S(2)}, u32[]{:S(2)}) collective-permute-start(bf16[512,128]{1,0:T(8,128)(2,1)S(1)} %constant_dynamic-slice_fusion.12), channel_id=1, source_target_pairs={{0,1},{1,0},{2,3},{3,2},{4,5},{5,4},{6,7},{7,6},{8,9},{9,8},{10,11... | collective-permute-start | bytes 393224 | tf_op jit(solution)/shard_map/ppermute | solution.py:185
  257.0 3.4 %copy-start.2 = (bf16[16,1024,256]{2,1,0:T(8,128)(2,1)S(1)}, bf16[16,1024,256]{2,1,0:T(8,128)(2,1)}, u32[]{:S(2)}) copy-start(bf16[16,1024,256]{2,1,0:T(8,128)(2,1)} %reshape.96.d_hbm) | copy-start | bytes 25165828
  260.3 2.8 slice-start.1
  263.1 21.6 %collective-permute-start.8 = (bf16[512,128]{1,0:T(8,128)(2,1)S(1)}, bf16[512,128]{1,0:T(8,128)(2,1)S(1)}, u32[]{:S(2)}, u32[]{:S(2)}) collective-permute-start(bf16[512,128]{1,0:T(8,128)(2,1)S(1)} %constant_dynamic-slice_fusion.10), channel_id=1, source_target_pairs={{0,1},{1,0},{2,3},{3,2},{4,5},{5,4},{6,7},{7,6},{8,9},{9,8},{10,11... | collective-permute-start | bytes 393224 | tf_op jit(solution)/shard_map/ppermute | solution.py:185
  263.2 3.4 %copy-start.4 = (bf16[1024,4096]{1,0:T(8,128)(2,1)S(1)}, bf16[1024,4096]{1,0:T(8,128)(2,1)}, u32[]{:S(2)}) copy-start(bf16[1024,4096]{1,0:T(8,128)(2,1)} %h_ref.1) | copy-start | bytes 25165828
  271.4 19.3 %collective-permute-start = (bf16[1024,128]{1,0:T(8,128)(2,1)S(1)}, bf16[1024,128]{1,0:T(8,128)(2,1)S(1)}, u32[]{:S(2)}, u32[]{:S(2)}) collective-permute-start(bf16[1024,128]{1,0:T(8,128)(2,1)S(1)} %constant_dynamic-slice_fusion.16), channel_id=1, source_target_pairs={{0,1},{1,0},{2,3},{3,2},{4,5},{5,4},{6,7},{7,6},{8,9},{9,8},{10,11... | collective-permute-start | bytes 786440 | tf_op jit(solution)/shard_map/ppermute | solution.py:185
  275.4 9.4 %collective-permute-start.15 = (bf16[512,128]{1,0:T(8,128)(2,1)S(1)}, bf16[512,128]{1,0:T(8,128)(2,1)S(1)}, u32[]{:S(2)}, u32[]{:S(2)}) collective-permute-start(bf16[512,128]{1,0:T(8,128)(2,1)S(1)} %constant_dynamic-slice_fusion.2), channel_id=1, source_target_pairs={{0,1},{1,0},{2,3},{3,2},{4,5},{5,4},{6,7},{7,6},{8,9},{9,8},{10,11... | collective-permute-start | bytes 393224 | tf_op jit(solution)/shard_map/ppermute | solution.py:185
  283.0 2.5 collective-permute-start.17
  284.5 4.0 %collective-permute-start.19 = (bf16[512,128]{1,0:T(8,128)(2,1)S(1)}, bf16[512,128]{1,0:T(8,128)(2,1)S(1)}, u32[]{:S(2)}, u32[]{:S(2)}) collective-permute-start(bf16[512,128]{1,0:T(8,128)(2,1)S(1)} %constant_dynamic-slice_fusion), channel_id=1, source_target_pairs={{0,1},{1,0},{2,3},{3,2},{4,5},{5,4},{6,7},{7,6},{8,9},{9,8},{10,11... | collective-permute-start | bytes 393224 | tf_op jit(solution)/shard_map/ppermute | solution.py:185
  284.7 6.0 %collective-permute-start.3 = (bf16[512,128]{1,0:T(8,128)(2,1)S(1)}, bf16[512,128]{1,0:T(8,128)(2,1)S(1)}, u32[]{:S(2)}, u32[]{:S(2)}) collective-permute-start(bf16[512,128]{1,0:T(8,128)(2,1)S(1)} %add_convert_fusion.8), channel_id=1, source_target_pairs={{0,2},{2,0},{4,6},{6,4},{8,10},{10,8},{12,14},{14,12},{1,3},{3,1},... | collective-permute-start | bytes 393224 | tf_op jit(solution)/shard_map/ppermute | solution.py:201
  284.8 9.3 %collective-permute-start.6 = (bf16[512,128]{1,0:T(8,128)(2,1)S(1)}, bf16[512,128]{1,0:T(8,128)(2,1)S(1)}, u32[]{:S(2)}, u32[]{:S(2)}) collective-permute-start(bf16[512,128]{1,0:T(8,128)(2,1)S(1)} %add_convert_fusion.7), channel_id=1, source_target_pairs={{0,4},{2,6},{4,0},{6,2},{8,12},{10,14},{12,8},{14,10},{1,5},{3,7},... | collective-permute-start | bytes 393224 | tf_op jit(solution)/shard_map/ppermute | solution.py:201
  285.6 9.9 %collective-permute-start.9 = (bf16[512,128]{1,0:T(8,128)(2,1)S(1)}, bf16[512,128]{1,0:T(8,128)(2,1)S(1)}, u32[]{:S(2)}, u32[]{:S(2)}) collective-permute-start(bf16[512,128]{1,0:T(8,128)(2,1)S(1)} %add_convert_fusion.6), channel_id=1, source_target_pairs={{0,6},{2,4},{4,2},{6,0},{8,14},{10,12},{12,10},{14,8},{1,7},{3,5},... | collective-permute-start | bytes 393224 | tf_op jit(solution)/shard_map/ppermute | solution.py:201
  288.5 7.9 %collective-permute-start.16 = (bf16[512,128]{1,0:T(8,128)(2,1)S(1)}, bf16[512,128]{1,0:T(8,128)(2,1)S(1)}, u32[]{:S(2)}, u32[]{:S(2)}) collective-permute-start(bf16[512,128]{1,0:T(8,128)(2,1)S(1)} %add_convert_fusion.4), channel_id=1, source_target_pairs={{0,2},{2,0},{4,6},{6,4},{8,10},{10,8},{12,14},{14,12},{1,3},{3,1},... | collective-permute-start | bytes 393224 | tf_op jit(solution)/shard_map/ppermute | solution.py:201
  290.6 9.1 %collective-permute-start.18 = (bf16[512,128]{1,0:T(8,128)(2,1)S(1)}, bf16[512,128]{1,0:T(8,128)(2,1)S(1)}, u32[]{:S(2)}, u32[]{:S(2)}) collective-permute-start(bf16[512,128]{1,0:T(8,128)(2,1)S(1)} %add_convert_fusion.3), channel_id=1, source_target_pairs={{0,4},{2,6},{4,0},{6,2},{8,12},{10,14},{12,8},{14,10},{1,5},{3,7},... | collective-permute-start | bytes 393224 | tf_op jit(solution)/shard_map/ppermute | solution.py:201
  290.6 9.9 %collective-permute-start.20 = (bf16[512,128]{1,0:T(8,128)(2,1)S(1)}, bf16[512,128]{1,0:T(8,128)(2,1)S(1)}, u32[]{:S(2)}, u32[]{:S(2)}) collective-permute-start(bf16[512,128]{1,0:T(8,128)(2,1)S(1)} %add_convert_fusion.2), channel_id=1, source_target_pairs={{0,6},{2,4},{4,2},{6,0},{8,14},{10,12},{12,10},{14,8},{1,7},{3,5},... | collective-permute-start | bytes 393224 | tf_op jit(solution)/shard_map/ppermute | solution.py:201
  300.6 1.4 collective-permute-start.21
  300.7 1.5 collective-permute-start.10

commit v4 on v3

--- a/solution.py
+++ b/solution.py
@@ -202,11 +202,11 @@
 
     lot = rows // LOTS
 
-    def share(o, c):
-        cut = lax.dynamic_slice(hidden_states, (c * lot, ((me ^ o) % team) * part), (lot, part))
+    def share(hidden, o, c):
+        cut = lax.dynamic_slice(hidden, (c * lot, ((me ^ o) % team) * part), (lot, part))
         return swap(cut, o)
 
-    early = [share(o, 0) for o in range(1, team)]
+    early = [share(hidden_states, o, 0) for o in range(1, team)]
     downs = send_call(team, teams, pool_down)
     downs, table = lax.optimization_barrier((downs, table))
     down_all = lax.all_to_all(
@@ -217,7 +217,8 @@
         tiled=True,
     )
 
-    late = [[share(o, c) for o in range(1, team)] for c in range(1, LOTS)]
+    early, hidden = lax.optimization_barrier((early, hidden_states))
+    late = [[share(hidden, o, c) for o in range(1, team)] for c in range(1, LOTS)]
 
     product = jnp.dot(
         hidden_states, kv_weight.reshape(width, 2 * kv_cols), preferred_element_type=F32
@@ -274,21 +275,23 @@
         return (keep.astype(F32) + other_core(give).astype(F32)).astype(BF16)
 
     own = over_cores(shrink_call(plans[0], needs[0], 0, hidden_states, column, down_all))
-    out = ()
+    shrunk = []
     per_lot = lot // TILE
     for c in range(LOTS):
-        total = own[c * lot : (c + 1) * lot].astype(F32)
+        one = {0: own[c * lot : (c + 1) * lot]}
         for o in range(1, team):
-            one = over_cores(shrink_call(plans[o], needs[o], c * per_lot, tokens[c][o - 1], zero, down_all))
-            total = total + swap(one, o).astype(F32)
-        shrunk = total.astype(BF16)
-        if cores == 2:
-            peer = other_core(shrunk)
-            shrunk = jnp.concatenate(
-                [jnp.where(core == 0, shrunk, peer), jnp.where(core == 0, peer, shrunk)], axis=1
-            )
-        out = grow_call(plans[0], needs[0] // held, c * per_lot, shrunk, ups, base_own, base_other, out)
-    keys, values = out
+            one[o] = over_cores(shrink_call(plans[o], needs[o], c * per_lot, tokens[c][o - 1], zero, down_all))
+        step = 1
+        while step < team:
+            got = {o: swap(one[o + step], step) for o in range(0, team, 2 * step)}
+            one = {o: (one[o].astype(F32) + x.astype(F32)).astype(BF16) for o, x in got.items()}
+            step *= 2
+        shrunk.append(one[0])
+    shrunk = jnp.concatenate(shrunk, axis=0)
+    if cores == 2:
+        peer = other_core(shrunk)
+        shrunk = jnp.concatenate([jnp.where(core == 0, shrunk, peer), jnp.where(core == 0, peer, shrunk)], axis=1)
+    keys, values = grow_call(plans[0], needs[0] // held, 0, shrunk, ups, base_own, base_other, ())
     return keys, values
 
 

time: 318 us -> 307 us (0.965); the launches traced: 312 us -> 306 us
  local copies, waits for them, and re-layouts: 65.6 us -> 60.5 us
    unnamed x30, local copies, waits for them, and re-layouts: 41 us -> 34.3 us
    pallas_call x2 -> x1, Pallas kernels: 9.86 us -> 7.14 us  [grow_call(): pl.pallas_call(functools.partial(grow_kernel, first), grid_spec=pltpu.Pre...]
    dynamic_slice x1 -> x2, local copies, waits for them, and re-layouts: 5.55 us -> 7.2 us  [share(): lax.dynamic_slice(hidden, (c * lot, (me ^ o) % team * part), (lot, part))]
  transfers between devices with their start and end apart: 25 -> 24, of which waited for: 13 -> 9; matrix products, arithmetic and copies ran while one was open for 24% -> 25% of each run, Pallas kernels for 9% -> 9%
where the time goes in v4:
time: 307 us; the launch traced here: 306 us
  waiting for transfers between devices  129 us (42%)
  local copies, waits for them, and re-layouts  60.5 us (20%)
  Pallas kernels  35 us (11%)
  starting transfers between devices  33.8 us (11%)
  matrix products  22.7 us (7%)
  between operations  16.3 us (5%)
  other arithmetic  8.63 us (3%)
    ppermute x12, waiting for transfers between devices, swap(): return lax.ppermute(x, 'replica', [(i, i ^ o) for i in range(replicas)])  127 us
    unnamed x30, local copies, waits for them, and re-layouts  34.3 us
    pallas_call x7, Pallas kernels, shrink_call(): pl.pallas_call(functools.partial(shrink_kernel, first), grid_spec=pltpu.P...  26.7 us
    dot_general x1, matrix products, per_device(): jnp.dot(hidden_states, kv_weight.reshape(width, 2 * kv_cols), preferred_e...  22.7 us
    reshape x1, local copies, waits for them, and re-layouts, per_device(): down_all = down_all.reshape(-1, part, 2 * rank_max)  14 us
    ppermute x12, starting transfers between devices, swap(): return lax.ppermute(x, 'replica', [(i, i ^ o) for i in range(replicas)])  14 us
    all_to_all x1, starting transfers between devices, per_device(): lax.all_to_all(jnp.tile(table, (replicas, 1)), 'replica', 0, 0, tiled=True)  7.25 us
    dynamic_slice x2, local copies, waits for them, and re-layouts, share(): lax.dynamic_slice(hidden, (c * lot, (me ^ o) % team * part), (lot, part))  7.2 us
  transfers between devices with their start and end apart: 24, of which 9 were waited for; matrix products, arithmetic and copies ran while one was open for 25% of the time, Pallas kernels for 9%

profile of v4, /device:TPU:0, one launch (start us, length us, event | category | flops | bytes accessed | tf_op | source)
XLA Modules:
  0.0 305.5 jit_solution(12145697942280875235)
XLA Ops:
  0.6 0.9 select_reduce_fusion.5
  1.5 0.7 pad_add_fusion
  2.8 7.3 %all-to-all-start = ((s32[8,1,16]{2,1,0:T(1,128)}), s32[8,1,16]{2,1,0:T(1,128)S(1)}, u32[]{:S(2)}, u32[]{:S(2)}) async-start(s32[8,1,16]{2,1,0:T(1,128)} %tile.2), calls=%async_computation | async-start | bytes 8192 | tf_op jit(solution)/shard_map/all_to_all | solution.py:190
  10.1 2.2 copy-done.3
  12.3 1.2 shard_map.95
  13.5 3.2 %copy-done.2 = bf16[2,4,2,1024,2,128]{5,4,3,2,1,0:T(2,128)(2,1)} copy-done((bf16[2,4,2,1024,2,128]{5,4,3,2,1,0:T(2,128)(2,1)}, bf16[2,4,2,1024,2,128]{5,4,3,2,1,0:T(2,128)(2,1)S(1)}, u32[]{:S(2)}) %copy-start.2) | copy-done | bytes 8388632
  16.7 6.0 %all-to-all-start.1 = ((bf16[16,1024,2,128]{3,2,1,0:T(2,128)(2,1)}), bf16[16,1024,2,128]{3,2,1,0:T(2,128)(2,1)}, u32[]{:S(2)}, u32[]{:S(2)}) async-start(bf16[16,1024,2,128]{3,2,1,0:T(2,128)(2,1)} %bitcast.77), calls=%async_computation.1 | async-start | bytes 16777216 | tf_op jit(solution)/shard_map/all_to_all | solution.py:212
  22.7 3.6 %constant_dynamic-slice_fusion.12 = (bf16[512,1024]{1,0:T(8,128)(2,1)}, bf16[512,1024]{1,0:T(8,128)(2,1)}, bf16[512,1024]{1,0:T(8,128)(2,1)}) fusion(bf16[1024,4096]{1,0:T(8,128)(2,1)} %h_ref.1, s32[]{:T(128)S(6)} %select_n.171, s32[]{:T(128)S(6)} %select_n.169, s32[]{:T(128)S(6)} %select_n.167), kind=kLoop, calls=%fused_computation.40 | loop fusion | bytes 6291468 | tf_op jit(solution)/shard_map/dynamic_slice | solution.py:206
  26.3 2.0 collective-permute-start.1
  28.3 1.5 collective-permute-start.2
  29.8 17.1 %copy.10 = bf16[512,8,2,1024]{3,1,2,0:T(8,128)(2,1)} copy(bf16[512,8,2,1024]{3,2,1,0:T(2,128)(2,1)} %bitcast.92) | data formatting | bytes 33554432
  46.9 22.7 %convolution_convert_fusion = bf16[1024,2048]{1,0:T(8,128)(2,1)S(1)} fusion(bf16[1024,4096]{1,0:T(8,128)(2,1)} %h_ref.1, bf16[4096,2048]{1,0:T(8,128)(2,1)} %bitcast.93), kind=kOutput, calls=%fused_computation | convolution fusion | flops 17181966336 | bytes 29360128 | tf_op jit(solution)/shard_map/dot_general | solution.py:223
  69.6 1.9 constant_dynamic-slice_fusion.9
  71.5 1.6 pad_maximum_fusion.1
  73.2 1.8 pad_maximum_fusion.own_ref
  93.3 20.5 %collective-permute-done.1.h_ref = bf16[512,1024]{1,0:T(8,128)(2,1)S(1)} collective-permute-done((bf16[512,1024]{1,0:T(8,128)(2,1)}, bf16[512,1024]{1,0:T(8,128)(2,1)S(1)}, u32[]{:S(2)}, u32[]{:S(2)}) %collective-permute-start.1) | collective-permute-done | bytes 1048608 | tf_op jit(solution)/shard_map/ppermute | solution.py:201
  113.8 68.5 %collective-permute-done.2.h_ref = bf16[512,1024]{1,0:T(8,128)(2,1)} collective-permute-done((bf16[512,1024]{1,0:T(8,128)(2,1)}, bf16[512,1024]{1,0:T(8,128)(2,1)}, u32[]{:S(2)}, u32[]{:S(2)}) %collective-permute-start.2) | collective-permute-done | bytes 1048608 | tf_op jit(solution)/shard_map/ppermute | solution.py:201
  182.3 20.7 %collective-permute-done.3.h_ref = bf16[512,1024]{1,0:T(8,128)(2,1)} collective-permute-done((bf16[512,1024]{1,0:T(8,128)(2,1)}, bf16[512,1024]{1,0:T(8,128)(2,1)}, u32[]{:S(2)}, u32[]{:S(2)}) %collective-permute-start.3) | collective-permute-done | bytes 1048608 | tf_op jit(solution)/shard_map/ppermute | solution.py:201
  203.0 3.6 %constant_dynamic-slice_fusion.20 = (bf16[512,1024]{1,0:T(8,128)(2,1)}, bf16[512,1024]{1,0:T(8,128)(2,1)}, bf16[512,1024]{1,0:T(8,128)(2,1)}) fusion(bf16[1024,4096]{1,0:T(8,128)(2,1)} %h_ref.1, s32[]{:T(128)S(6)} %select_n.167, s32[]{:T(128)S(6)} %select_n.171, s32[]{:T(128)S(6)} %select_n.169), kind=kLoop, calls=%fused_computation.83 | loop fusion | bytes 6291468 | tf_op jit(solution)/shard_map/dynamic_slice | solution.py:206
  206.6 3.4 %collective-permute-start.16 = (bf16[512,1024]{1,0:T(8,128)(2,1)}, bf16[512,1024]{1,0:T(8,128)(2,1)}, u32[]{:S(2)}, u32[]{:S(2)}) collective-permute-start(bf16[512,1024]{1,0:T(8,128)(2,1)} %get-tuple-element.41), channel_id=1, source_target_pairs={{0,6},{2,4},{4,2},{6,0},{8,14},{10,12},{12,10},{14,8},{1,7},{3,5},... | collective-permute-start | bytes 3145736 | tf_op jit(solution)/shard_map/ppermute | solution.py:201
  210.4 1.5 collective-permute-start.11
  211.8 14.0 %reshape.96.d_hbm = bf16[16,1024,256]{2,1,0:T(8,128)(2,1)} reshape(bf16[16,1024,2,128]{3,2,1,0:T(2,128)(2,1)} %all-to-all-done.1) | data formatting | bytes 16777216 | tf_op jit(solution)/shard_map/reshape | solution.py:253
  225.9 3.4 %copy-done = bf16[16,1024,256]{2,1,0:T(8,128)(2,1)S(1)} copy-done((bf16[16,1024,256]{2,1,0:T(8,128)(2,1)S(1)}, bf16[16,1024,256]{2,1,0:T(8,128)(2,1)}, u32[]{:S(2)}) %copy-start) | copy-done | bytes 8388632
  229.3 3.5 %shard_map.99 = bf16[512,256]{1,0:T(8,128)(2,1)S(1)} custom-call(s32[4]{0:T(128)S(1)} %get-tuple-element.77.low, s32[4]{0:T(128)S(1)} %get-tuple-element.34.high, s32[8]{0:T(128)S(1)} %bitcast_subtract_fusion.begin, s32[8]{0:T(128)S(1)} %bitcast.90, s32[8]{0:T(128)S(1)} %get-tuple-element.31.rank, f32[8]{0:T(128)S(1)} %convert_rsqrt_fusion.scale, ...), custom_call_target="tpu_custom_call" | custom-call | flops 536870912 | bytes 2097152 | tf_op jit(solution)/shard_map/pallas_call | solution.py:67
  233.4 0.7 dynamic-slice_dynamic-update-slice_fusion.7
  234.2 0.7 dynamic-slice_dynamic-update-slice_fusion.6
  234.9 0.7 dynamic-slice_dynamic-update-slice_fusion.5
  235.6 0.7 dynamic-slice_dynamic-update-slice_fusion.4
  236.3 0.7 dynamic-slice_dynamic-update-slice_fusion.3
  238.5 0.7 dynamic-slice_dynamic-update-slice_fusion
  239.2 4.5 %all-to-all-start.2 = ((bf16[8,2,128,512]{3,2,1,0:T(8,128)(2,1)}), bf16[8,2,128,512]{3,2,1,0:T(8,128)(2,1)}, u32[]{:S(2)}, u32[]{:S(2)}) async-start(bf16[8,2,128,512]{3,2,1,0:T(8,128)(2,1)} %dynamic-slice_dynamic-update-slice_fusion), calls=%async_computation.2 | async-start | bytes 4194304 | tf_op jit(solution)/shard_map/all_to_all | solution.py:254
  243.8 3.4 %copy-done.1 = bf16[16,1024,256]{2,1,0:T(8,128)(2,1)S(1)} copy-done((bf16[16,1024,256]{2,1,0:T(8,128)(2,1)S(1)}, bf16[16,1024,256]{2,1,0:T(8,128)(2,1)}, u32[]{:S(2)}) %copy-start.1) | copy-done | bytes 8388632
  247.1 4.5 %shard_map.98 = bf16[512,256]{1,0:T(8,128)(2,1)S(1)} custom-call(s32[4]{0:T(128)S(1)} %get-tuple-element.78.low, s32[4]{0:T(128)S(1)} %get-tuple-element.33.high, s32[8]{0:T(128)S(1)} %bitcast_subtract_fusion.2.begin, s32[8]{0:T(128)S(1)} %bitcast.87, s32[8]{0:T(128)S(1)} %get-tuple-element.30.rank, f32[8]{0:T(128)S(1)} %convert_rsqrt_fusion.1.scale, ...), custom_call_target="tpu_custom_call" | custom-call | flops 536870912 | bytes 2097152 | tf_op jit(solution)/shard_map/pallas_call | solution.py:67
  252.2 2.1 shard_map.97
  254.5 4.5 %shard_map.102 = bf16[512,256]{1,0:T(8,128)(2,1)S(1)} custom-call(s32[4]{0:T(128)S(1)} %get-tuple-element.77.low, s32[4]{0:T(128)S(1)} %get-tuple-element.34.high, s32[8]{0:T(128)S(1)} %bitcast_subtract_fusion.begin, s32[8]{0:T(128)S(1)} %bitcast.91, s32[8]{0:T(128)S(1)} %get-tuple-element.31.rank, f32[8]{0:T(128)S(1)} %convert_rsqrt_fusion.scale, ...), custom_call_target="tpu_custom_call" | custom-call | flops 536870912 | bytes 2097152 | tf_op jit(solution)/shard_map/pallas_call | solution.py:67
  259.0 4.7 %shard_map.96 = bf16[1024,256]{1,0:T(8,128)(2,1)S(1)} custom-call(s32[4]{0:T(128)S(1)} %get-tuple-element.76.low, s32[4]{0:T(128)S(1)} %get-tuple-element.35.high, s32[8]{0:T(128)S(1)} %get-tuple-element.75.begin, s32[8]{0:T(128)S(1)} %bitcast.81, s32[8]{0:T(128)S(1)} %get-tuple-element.28.rank, f32[8]{0:T(128)S(1)} %convert_rsqrt_fusion.3.scale, ...), custom_call_target="tpu_custom_call" | custom-call | flops 1073741824 | bytes 4194304 | tf_op jit(solution)/shard_map/pallas_call | solution.py:67
  264.0 3.1 %shard_map.101 = bf16[512,256]{1,0:T(8,128)(2,1)S(1)} custom-call(s32[4]{0:T(128)S(1)} %get-tuple-element.78.low, s32[4]{0:T(128)S(1)} %get-tuple-element.33.high, s32[8]{0:T(128)S(1)} %bitcast_subtract_fusion.2.begin, s32[8]{0:T(128)S(1)} %bitcast.88, s32[8]{0:T(128)S(1)} %get-tuple-element.30.rank, f32[8]{0:T(128)S(1)} %convert_rsqrt_fusion.1.scale, ...), custom_call_target="tpu_custom_call" | custom-call | flops 536870912 | bytes 2097152 | tf_op jit(solution)/shard_map/pallas_call | solution.py:67
  267.7 4.2 %shard_map.100 = bf16[512,256]{1,0:T(8,128)(2,1)S(1)} custom-call(s32[4]{0:T(128)S(1)} %get-tuple-element.79.low, s32[4]{0:T(128)S(1)} %get-tuple-element.32.high, s32[8]{0:T(128)S(1)} %bitcast_subtract_fusion.4.begin, s32[8]{0:T(128)S(1)} %bitcast.85, s32[8]{0:T(128)S(1)} %get-tuple-element.29.rank, f32[8]{0:T(128)S(1)} %convert_rsqrt_fusion.2.scale, ...), custom_call_target="tpu_custom_call" | custom-call | flops 536870912 | bytes 2097152 | tf_op jit(solution)/shard_map/pallas_call | solution.py:67
  272.1 0.9 add_convert_fusion.9
  274.5 1.3 collective-permute-start.6
  275.8 0.8 collective-permute-start.18
  276.7 6.1 %collective-permute-done.9 = bf16[512,128]{1,0:T(8,128)(2,1)S(1)} collective-permute-done((bf16[512,128]{1,0:T(8,128)(2,1)S(1)}, bf16[512,128]{1,0:T(8,128)(2,1)S(1)}, u32[]{:S(2)}, u32[]{:S(2)}) %collective-permute-start.9) | collective-permute-done | bytes 131104 | tf_op jit(solution)/shard_map/ppermute | solution.py:201
  282.8 1.9 collective-permute-start.10
  284.8 6.6 %collective-permute-done.18 = bf16[512,128]{1,0:T(8,128)(2,1)S(1)} collective-permute-done((bf16[512,128]{1,0:T(8,128)(2,1)S(1)}, bf16[512,128]{1,0:T(8,128)(2,1)S(1)}, u32[]{:S(2)}, u32[]{:S(2)}) %collective-permute-start.18) | collective-permute-done | bytes 131104 | tf_op jit(solution)/shard_map/ppermute | solution.py:201
  292.1 1.5 collective-permute-done.13
  293.6 2.9 collective-permute-done.19
  296.7 1.5 collective-permute-done.20
  298.4 7.1 %shard_map.103 = (bf16[1024,512]{1,0:T(8,128)(2,1)}, bf16[1024,512]{1,0:T(8,128)(2,1)}) custom-call(s32[4]{0:T(128)S(1)} %get-tuple-element.76.low, s32[4]{0:T(128)S(1)} %get-tuple-element.35.high, s32[8]{0:T(128)S(1)} %get-tuple-element.75.begin, s32[8]{0:T(128)S(1)} %bitcast.82, s32[8]{0:T(128)S(1)} %get-tuple-element.74.slot, ...), custom_call_target="tpu_custom_call" | custom-call | flops 536870912 | bytes 6291456 | tf_op jit(solution)/shard_map/pallas_call | solution.py:120
  (98 shorter events, 10.5 us)
Async XLA Ops:
  2.8 13.9 %all-to-all-start = ((s32[8,1,16]{2,1,0:T(1,128)}), s32[8,1,16]{2,1,0:T(1,128)S(1)}, u32[]{:S(2)}, u32[]{:S(2)}) async-start(s32[8,1,16]{2,1,0:T(1,128)} %tile.2), calls=%async_computation | async-start | bytes 8192 | tf_op jit(solution)/shard_map/all_to_all | solution.py:190
  10.1 2.2 copy-start.3
  13.5 3.2 %copy-start.2 = (bf16[2,4,2,1024,2,128]{5,4,3,2,1,0:T(2,128)(2,1)}, bf16[2,4,2,1024,2,128]{5,4,3,2,1,0:T(2,128)(2,1)S(1)}, u32[]{:S(2)}) copy-start(bf16[2,4,2,1024,2,128]{5,4,3,2,1,0:T(2,128)(2,1)S(1)} %shard_map.95) | copy-start | bytes 25165828
  16.7 195.1 %all-to-all-start.1 = ((bf16[16,1024,2,128]{3,2,1,0:T(2,128)(2,1)}), bf16[16,1024,2,128]{3,2,1,0:T(2,128)(2,1)}, u32[]{:S(2)}, u32[]{:S(2)}) async-start(bf16[16,1024,2,128]{3,2,1,0:T(2,128)(2,1)} %bitcast.77), calls=%async_computation.1 | async-start | bytes 16777216 | tf_op jit(solution)/shard_map/all_to_all | solution.py:212
  26.3 87.5 %collective-permute-start.1 = (bf16[512,1024]{1,0:T(8,128)(2,1)}, bf16[512,1024]{1,0:T(8,128)(2,1)S(1)}, u32[]{:S(2)}, u32[]{:S(2)}) collective-permute-start(bf16[512,1024]{1,0:T(8,128)(2,1)} %get-tuple-element.45), channel_id=1, source_target_pairs={{0,2},{2,0},{4,6},{6,4},{8,10},{10,8},{12,14},{14,12},{1,3},{3,1},... | collective-permute-start | bytes 3145736 | tf_op jit(solution)/shard_map/ppermute | solution.py:201
  28.3 154.0 %collective-permute-start.2 = (bf16[512,1024]{1,0:T(8,128)(2,1)}, bf16[512,1024]{1,0:T(8,128)(2,1)}, u32[]{:S(2)}, u32[]{:S(2)}) collective-permute-start(bf16[512,1024]{1,0:T(8,128)(2,1)} %get-tuple-element.44), channel_id=1, source_target_pairs={{0,4},{2,6},{4,0},{6,2},{8,12},{10,14},{12,8},{14,10},{1,5},{3,7},... | collective-permute-start | bytes 3145736 | tf_op jit(solution)/shard_map/ppermute | solution.py:201
  29.8 173.2 %collective-permute-start.3 = (bf16[512,1024]{1,0:T(8,128)(2,1)}, bf16[512,1024]{1,0:T(8,128)(2,1)}, u32[]{:S(2)}, u32[]{:S(2)}) collective-permute-start(bf16[512,1024]{1,0:T(8,128)(2,1)} %get-tuple-element.43), channel_id=1, source_target_pairs={{0,6},{2,4},{4,2},{6,0},{8,14},{10,12},{12,10},{14,8},{1,7},{3,5},... | collective-permute-start | bytes 3145736 | tf_op jit(solution)/shard_map/ppermute | solution.py:201
  71.5 1.6 copy-start.5
  71.5 1.6 copy-start.6
  73.1 138.7 %collective-permute-start.4 = (bf16[1024,1024]{1,0:T(8,128)(2,1)}, bf16[1024,1024]{1,0:T(8,128)(2,1)}, u32[]{:S(2)}, u32[]{:S(2)}) collective-permute-start(bf16[1024,1024]{1,0:T(8,128)(2,1)} %pad_maximum_fusion.1), channel_id=1, source_target_pairs={{0,1},{1,0},{2,3},{3,2},{4,5},{5,4},{6,7},{7,6},{8,9},{9,8},{10,11... | collective-permute-start | bytes 6291464 | tf_op jit(solution)/shard_map/ppermute | solution.py:185
  206.6 47.8 %collective-permute-start.16 = (bf16[512,1024]{1,0:T(8,128)(2,1)}, bf16[512,1024]{1,0:T(8,128)(2,1)}, u32[]{:S(2)}, u32[]{:S(2)}) collective-permute-start(bf16[512,1024]{1,0:T(8,128)(2,1)} %get-tuple-element.41), channel_id=1, source_target_pairs={{0,6},{2,4},{4,2},{6,0},{8,14},{10,12},{12,10},{14,8},{1,7},{3,5},... | collective-permute-start | bytes 3145736 | tf_op jit(solution)/shard_map/ppermute | solution.py:201
  210.0 53.9 %collective-permute-start.14 = (bf16[512,1024]{1,0:T(8,128)(2,1)}, bf16[512,1024]{1,0:T(8,128)(2,1)}, u32[]{:S(2)}, u32[]{:S(2)}) collective-permute-start(bf16[512,1024]{1,0:T(8,128)(2,1)} %get-tuple-element.42), channel_id=1, source_target_pairs={{0,4},{2,6},{4,0},{6,2},{8,12},{10,14},{12,8},{14,10},{1,5},{3,7},... | collective-permute-start | bytes 3145736 | tf_op jit(solution)/shard_map/ppermute | solution.py:201
  210.4 56.9 %collective-permute-start.11 = (bf16[512,1024]{1,0:T(8,128)(2,1)}, bf16[512,1024]{1,0:T(8,128)(2,1)}, u32[]{:S(2)}, u32[]{:S(2)}) collective-permute-start(bf16[512,1024]{1,0:T(8,128)(2,1)} %get-tuple-element.40), channel_id=1, source_target_pairs={{0,2},{2,0},{4,6},{6,4},{8,10},{10,8},{12,14},{14,12},{1,3},{3,1},... | collective-permute-start | bytes 3145736 | tf_op jit(solution)/shard_map/ppermute | solution.py:201
  225.9 3.4 %copy-start = (bf16[16,1024,256]{2,1,0:T(8,128)(2,1)S(1)}, bf16[16,1024,256]{2,1,0:T(8,128)(2,1)}, u32[]{:S(2)}) copy-start(bf16[16,1024,256]{2,1,0:T(8,128)(2,1)} %reshape.96.d_hbm) | copy-start | bytes 25165828
  229.2 4.2 %copy-start.4 = (bf16[2,2,128,512]{3,2,1,0:T(8,128)(2,1)S(1)}, bf16[2,2,128,512]{3,2,1,0:T(8,128)(2,1)}, u32[]{:S(2)}) copy-start(bf16[2,2,128,512]{3,2,1,0:T(8,128)(2,1)} %param.11) | copy-start | bytes 1572868
  233.4 38.5 %collective-permute-start.8 = (bf16[512,128]{1,0:T(8,128)(2,1)}, bf16[512,128]{1,0:T(8,128)(2,1)}, u32[]{:S(2)}, u32[]{:S(2)}) collective-permute-start(bf16[512,128]{1,0:T(8,128)(2,1)} %constant_dynamic-slice_fusion.3), channel_id=1, source_target_pairs={{0,1},{1,0},{2,3},{3,2},{4,5},{5,4},{6,7},{7,6},{8,9},{9,8},{10,11... | collective-permute-start | bytes 393224 | tf_op jit(solution)/shard_map/ppermute | solution.py:185
  239.2 59.2 %all-to-all-start.2 = ((bf16[8,2,128,512]{3,2,1,0:T(8,128)(2,1)}), bf16[8,2,128,512]{3,2,1,0:T(8,128)(2,1)}, u32[]{:S(2)}, u32[]{:S(2)}) async-start(bf16[8,2,128,512]{3,2,1,0:T(8,128)(2,1)} %dynamic-slice_dynamic-update-slice_fusion), calls=%async_computation.2 | async-start | bytes 4194304 | tf_op jit(solution)/shard_map/all_to_all | solution.py:254
  243.7 3.4 %copy-start.1 = (bf16[16,1024,256]{2,1,0:T(8,128)(2,1)S(1)}, bf16[16,1024,256]{2,1,0:T(8,128)(2,1)}, u32[]{:S(2)}) copy-start(bf16[16,1024,256]{2,1,0:T(8,128)(2,1)} %reshape.96.d_hbm) | copy-start | bytes 25165828
  247.1 7.4 %slice-start = ((s8[8388608]{0:T(1024)(128)(4,1)}), s8[4194304]{0:T(1024)(128)(4,1)S(1)}, s32[]{:S(2)}) async-start(s8[8388608]{0:T(1024)(128)(4,1)} %bitcast.75), calls=%async_computation.3 | async-start | bytes 8388608
  251.7 24.2 %collective-permute-start.7 = (bf16[512,128]{1,0:T(8,128)(2,1)S(1)}, bf16[512,128]{1,0:T(8,128)(2,1)S(1)}, u32[]{:S(2)}, u32[]{:S(2)}) collective-permute-start(bf16[512,128]{1,0:T(8,128)(2,1)S(1)} %constant_dynamic-slice_fusion.5), channel_id=1, source_target_pairs={{0,1},{1,0},{2,3},{3,2},{4,5},{5,4},{6,7},{7,6},{8,9},{9,8},{10,11... | collective-permute-start | bytes 393224 | tf_op jit(solution)/shard_map/ppermute | solution.py:185
  252.2 2.3 slice-start.1
  252.2 6.8 %slice-start.2 = ((s8[8388608]{0:T(1024)(128)(4,1)}), s8[4194304]{0:T(1024)(128)(4,1)S(1)}, s32[]{:S(2)}) async-start(s8[8388608]{0:T(1024)(128)(4,1)} %bitcast.78), calls=%async_computation.5 | async-start | bytes 8388608
  254.3 4.7 %slice-start.3 = ((s8[8388608]{0:T(1024)(128)(4,1)}), s8[4194304]{0:T(1024)(128)(4,1)S(1)}, s32[]{:S(2)}) async-start(s8[8388608]{0:T(1024)(128)(4,1)} %bitcast.78), calls=%async_computation.6 | async-start | bytes 8388608
  254.4 18.7 %collective-permute-start.5 = (bf16[512,128]{1,0:T(8,128)(2,1)S(1)}, bf16[512,128]{1,0:T(8,128)(2,1)S(1)}, u32[]{:S(2)}, u32[]{:S(2)}) collective-permute-start(bf16[512,128]{1,0:T(8,128)(2,1)S(1)} %constant_dynamic-slice_fusion.7), channel_id=1, source_target_pairs={{0,1},{1,0},{2,3},{3,2},{4,5},{5,4},{6,7},{7,6},{8,9},{9,8},{10,11... | collective-permute-start | bytes 393224 | tf_op jit(solution)/shard_map/ppermute | solution.py:185
  263.8 28.2 %collective-permute-start = (bf16[1024,128]{1,0:T(8,128)(2,1)S(1)}, bf16[1024,128]{1,0:T(8,128)(2,1)S(1)}, u32[]{:S(2)}, u32[]{:S(2)}) collective-permute-start(bf16[1024,128]{1,0:T(8,128)(2,1)S(1)} %constant_dynamic-slice_fusion.16), channel_id=1, source_target_pairs={{0,1},{1,0},{2,3},{3,2},{4,5},{5,4},{6,7},{7,6},{8,9},{9,8},{10,11... | collective-permute-start | bytes 786440 | tf_op jit(solution)/shard_map/ppermute | solution.py:185
  267.3 6.3 %collective-permute-start.17 = (bf16[512,128]{1,0:T(8,128)(2,1)S(1)}, bf16[512,128]{1,0:T(8,128)(2,1)S(1)}, u32[]{:S(2)}, u32[]{:S(2)}) collective-permute-start(bf16[512,128]{1,0:T(8,128)(2,1)S(1)} %constant_dynamic-slice_fusion), channel_id=1, source_target_pairs={{0,1},{1,0},{2,3},{3,2},{4,5},{5,4},{6,7},{7,6},{8,9},{9,8},{10,11... | collective-permute-start | bytes 393224 | tf_op jit(solution)/shard_map/ppermute | solution.py:185
  271.9 10.9 %collective-permute-start.15 = (bf16[512,128]{1,0:T(8,128)(2,1)S(1)}, bf16[512,128]{1,0:T(8,128)(2,1)S(1)}, u32[]{:S(2)}, u32[]{:S(2)}) collective-permute-start(bf16[512,128]{1,0:T(8,128)(2,1)S(1)} %constant_dynamic-slice_fusion.1), channel_id=1, source_target_pairs={{0,1},{1,0},{2,3},{3,2},{4,5},{5,4},{6,7},{7,6},{8,9},{9,8},{10,11... | collective-permute-start | bytes 393224 | tf_op jit(solution)/shard_map/ppermute | solution.py:185
  273.1 1.4 collective-permute-start.12
  273.6 9.2 %collective-permute-start.9 = (bf16[512,128]{1,0:T(8,128)(2,1)S(1)}, bf16[512,128]{1,0:T(8,128)(2,1)S(1)}, u32[]{:S(2)}, u32[]{:S(2)}) collective-permute-start(bf16[512,128]{1,0:T(8,128)(2,1)S(1)} %add_convert_fusion.9), channel_id=1, source_target_pairs={{0,2},{2,0},{4,6},{6,4},{8,10},{10,8},{12,14},{14,12},{1,3},{3,1},... | collective-permute-start | bytes 393224 | tf_op jit(solution)/shard_map/ppermute | solution.py:201
  274.5 17.6 %collective-permute-start.6 = (bf16[512,128]{1,0:T(8,128)(2,1)S(1)}, bf16[512,128]{1,0:T(8,128)(2,1)S(1)}, u32[]{:S(2)}, u32[]{:S(2)}) collective-permute-start(bf16[512,128]{1,0:T(8,128)(2,1)S(1)} %add_convert_fusion.12), channel_id=1, source_target_pairs={{0,2},{2,0},{4,6},{6,4},{8,10},{10,8},{12,14},{14,12},{1,3},{3,1},... | collective-permute-start | bytes 393224 | tf_op jit(solution)/shard_map/ppermute | solution.py:201
  275.8 15.5 %collective-permute-start.18 = (bf16[512,128]{1,0:T(8,128)(2,1)S(1)}, bf16[512,128]{1,0:T(8,128)(2,1)S(1)}, u32[]{:S(2)}, u32[]{:S(2)}) collective-permute-start(bf16[512,128]{1,0:T(8,128)(2,1)S(1)} %add_convert_fusion.3), channel_id=1, source_target_pairs={{0,2},{2,0},{4,6},{6,4},{8,10},{10,8},{12,14},{14,12},{1,3},{3,1},... | collective-permute-start | bytes 393224 | tf_op jit(solution)/shard_map/ppermute | solution.py:201
  282.8 10.8 %collective-permute-start.13 = (bf16[512,128]{1,0:T(8,128)(2,1)S(1)}, bf16[512,128]{1,0:T(8,128)(2,1)S(1)}, u32[]{:S(2)}, u32[]{:S(2)}) collective-permute-start(bf16[512,128]{1,0:T(8,128)(2,1)S(1)} %add_convert_fusion.6), channel_id=1, source_target_pairs={{0,2},{2,0},{4,6},{6,4},{8,10},{10,8},{12,14},{14,12},{1,3},{3,1},... | collective-permute-start | bytes 393224 | tf_op jit(solution)/shard_map/ppermute | solution.py:201
  282.8 10.7 %collective-permute-start.10 = (bf16[512,128]{1,0:T(8,128)(2,1)S(1)}, bf16[512,128]{1,0:T(8,128)(2,1)S(1)}, u32[]{:S(2)}, u32[]{:S(2)}) collective-permute-start(bf16[512,128]{1,0:T(8,128)(2,1)S(1)} %add_convert_fusion.8), channel_id=1, source_target_pairs={{0,4},{2,6},{4,0},{6,2},{8,12},{10,14},{12,8},{14,10},{1,5},{3,7},... | collective-permute-start | bytes 393224 | tf_op jit(solution)/shard_map/ppermute | solution.py:201
  291.4 5.0 %collective-permute-start.19 = (bf16[512,128]{1,0:T(8,128)(2,1)S(1)}, bf16[512,128]{1,0:T(8,128)(2,1)S(1)}, u32[]{:S(2)}, u32[]{:S(2)}) collective-permute-start(bf16[512,128]{1,0:T(8,128)(2,1)S(1)} %add_convert_fusion.2), channel_id=1, source_target_pairs={{0,4},{2,6},{4,0},{6,2},{8,12},{10,14},{12,8},{14,10},{1,5},{3,7},... | collective-permute-start | bytes 393224 | tf_op jit(solution)/shard_map/ppermute | solution.py:201
  296.6 1.6 collective-permute-start.20
